TPU v7x, 512 devices: a whole 4x8x8 slice. The times are simulated.
512 devices in a mesh: grid: 64 (over z_hi, y, core), comp: 8 (over x, z_lo).
Axes of the slice: x: 4, y: 8, z: 8 (z_hi: 4, z_lo: 2; z = z_hi * 2 + z_lo), core: 2. Of those that a mesh axis runs over, the one named last changes fastest.
Arguments:
- fields_runs: bfloat16 [1024, 131072], P('comp', 'grid'), may hold values from -16 to 16
- eof_basis: bfloat16 [131072, 512], P('grid', 'comp'), may hold values from -6 to 6
- weights_inv: float32 [1024, 1024], P(None, 'grid'), may hold values from -1 to 1
- design: float32 [8, 1024], replicated, may hold values from 0 to 1
- new_settings: float32 [8, 2048], replicated, may hold values from 0 to 1
- lscale: float32 [8, 512], P(None, 'comp'), may hold values from 0.5 to 4
- variance: float32 [512], P('comp'), may hold values from 0.5 to 2
Outputs:
- imitated: bfloat16 [2048, 131072], P('comp', 'grid')
All inputs are finite; a program needn't handle non-finite values.
Results may differ from a plain program's by a relative error of at most 0.0049.
Values may be sent and summed in bfloat16 or wider, within the bound.
No kernel may reach another device: no remote copies, remote signals or barrier semaphores. Data moves between devices by JAX's collectives and lax.ppermute only.
A program may use at most 64 MiB of HBM per device.

v0:
```python
import math

import jax
import jax.numpy as jnp
from jax import lax
from jax.sharding import PartitionSpec as P

SQRT_THREE = 1.7320508075688772


def matern_block(lscale, variance, alpha, settings, design):
    kblock = lscale.shape[1]
    sq = jnp.zeros((kblock, settings.shape[1], design.shape[1]), jnp.float32)
    for param in range(lscale.shape[0]):
        diff = settings[param][:, None] - design[param][None, :]
        sq = sq + (diff[None, :, :] / lscale[param][:, None, None]) ** 2
    radius = jnp.sqrt(sq)
    cross = variance[:, None, None] * (1.0 + SQRT_THREE * radius) * jnp.exp(-SQRT_THREE * radius)
    return jnp.einsum("kni,ik->nk", cross, alpha, precision=lax.Precision.HIGHEST)


def on_device(fields_runs, eof_basis, weights_inv, design, new_settings, lscale, variance):
    grid_count = lax.axis_size("grid")
    comp_count = lax.axis_size("comp")
    grid_place = lax.axis_index("grid")
    cell_local = eof_basis.shape[0]
    comps_total = eof_basis.shape[1] * comp_count
    project_scale = 1.0 / math.sqrt(cell_local * grid_count)
    partial_coef = (
        jnp.dot(
            lax.all_gather(fields_runs, "comp", axis=0, tiled=True),
            eof_basis,
            preferred_element_type=jnp.float32,
        )
        * project_scale
    )
    coef_rows = lax.psum_scatter(partial_coef, "grid", scatter_dimension=0, tiled=True)
    alpha_part = jnp.dot(
        weights_inv, coef_rows, precision=lax.Precision.HIGHEST, preferred_element_type=jnp.float32
    )
    alpha = lax.psum(alpha_part, "grid")
    params = new_settings.shape[0]
    new_local = new_settings.shape[1] // grid_count
    per_block = new_local // comp_count
    shaped = new_settings.reshape(params, comp_count, grid_count, per_block)
    chosen = lax.dynamic_index_in_dim(shaped, grid_place, 2, keepdims=False).reshape(
        params, new_local
    )
    pred_local = matern_block(lscale, variance, alpha, chosen, design).astype(jnp.bfloat16)
    swapped = lax.all_to_all(pred_local, "comp", split_axis=0, concat_axis=1, tiled=True)
    pred_block = lax.all_gather(swapped, "grid", axis=0, tiled=True)
    recon_scale = 1.0 / math.sqrt(comps_total)
    summed = lax.dot_general(
        pred_block,
        lax.all_gather(eof_basis, "comp", axis=1, tiled=True),
        (((1,), (1,)), ((), ())),
        preferred_element_type=jnp.float32,
    )
    return (summed * recon_scale).astype(jnp.bfloat16)


def solution(mesh):
    placed = (
        P("comp", "grid"),
        P("grid", "comp"),
        P(None, "grid"),
        P(),
        P(),
        P(None, "comp"),
        P("comp"),
    )
    return jax.shard_map(
        on_device, mesh=mesh, in_specs=placed, out_specs=P("comp", "grid"), check_vma=False
    )
```

profile of v0, /device:TPU:1, one launch (start us, length us, event | category | flops | bytes accessed | tf_op | source)
XLA Modules:
  0.0 892.4 jit_solution(7276861449839407683)
XLA Ops:
  6.5 0.0 copy-start
  6.5 0.0 copy-start.3
  6.5 0.0 copy-start.2
  6.5 0.0 copy-start.1
  6.5 0.0 all-gather.4.cloned.1.call-start
  6.6 0.7 all-gather.4.cloned.1.call-update
  7.3 0.0 copy-start.4
  7.3 0.0 reduce-scatter.2.cloned.1.call-start
  7.3 103.6 %all-gather.4.cloned.1.call-done = bf16[1024,2048]{1,0:T(8,128)(2,1)} async-done(((bf16[128,2048]{1,0:T(8,128)(2,1)}), bf16[1024,2048]{1,0:T(8,128)(2,1)}) %all-gather.4.cloned.1.call-update) | async-done | bytes 4194320 | tf_op jit(solution)/shard_map/all_gather | solution.py:31
  110.9 4.2 convolution_multiply_fusion.1
  115.2 0.0 reduce-scatter.2.cloned.1.call-update
  115.2 0.0 all-reduce.2.cloned.1.call-start
  115.2 144.4 %reduce-scatter.2.cloned.1.call-done = f32[16,64]{1,0:T(8,128)} async-done(((f32[1024,64]{1,0:T(8,128)}), f32[16,64]{1,0:T(8,128)}) %reduce-scatter.2.cloned.1.call-update) | async-done | bytes 4112 | tf_op jit(solution)/shard_map/reduce_scatter | solution.py:37
  259.6 0.0 copy-done
  259.6 1.8 convolution_bitcast_fusion
  261.4 0.0 all-reduce.2.cloned.1.call-update
  261.5 0.0 all-gather.6.cloned.1.call-start
  261.5 0.5 all-gather.6.cloned.1.call-update
  262.1 0.0 copy-done.3
  262.1 0.0 copy-done.2
  262.1 0.0 copy-done.1
  262.1 0.3 copy.11
  262.5 0.3 dynamic-slice_reduce_fusion.7
  262.7 0.1 sub.152
  262.8 0.1 sub.176
  262.9 0.1 sub.172
  263.0 0.1 sub.168
  263.1 0.1 sub.164
  263.1 0.1 sub.160
  263.2 0.1 sub.156
  263.3 0.1 sub.180
  263.4 0.1 broadcast_subtract_fusion
  263.5 0.1 broadcast_subtract_fusion.6
  263.6 0.1 broadcast_subtract_fusion.4
  263.7 0.1 broadcast_subtract_fusion.2
  263.8 509.3 %all-reduce.2.cloned.1.call-done = f32[1024,64]{0,1:T(8,128)} async-done(((f32[1024,64]{0,1:T(8,128)}), f32[1024,64]{0,1:T(8,128)}) %all-reduce.2.cloned.1.call-update) | async-done | bytes 262160 | tf_op jit(solution)/shard_map/psum | solution.py:41
  773.1 0.0 copy-done.4
  773.1 17.9 %fusion.8 = bf16[64,1,32]{2,1,0:T(2,128)(2,1)S(1)} fusion(f32[64]{0:T(128)S(1)} %get-tuple-element.27, f32[32,1024]{1,0:T(8,128)S(1)} %get-tuple-element.29, f32[64]{0:T(128)S(1)} %get-tuple-element.28, f32[32,1024]{1,0:T(8,128)S(1)} %get-tuple-element.30, f32[64]{0:T(128)S(1)} %get-tuple-element.22, f32[32,1024]{1,0:T(8,128)S(1)} %get-tuple-element.31, ...), kind=kOutput, calls=%fused_computation.16 | convolution fusion | flops 83886080 | bytes 1317120 | tf_op jit(solution)/shard_map/kni,ik->nk/dot_general | solution.py:19
  791.0 0.1 copy.14
  791.0 0.1 reshape.295
  791.1 9.0 %all_to_all.19 = bf16[8,2,128]{2,1,0:T(2,128)(2,1)S(1)} all-to-all(bf16[8,2,128]{2,1,0:T(2,128)(2,1)S(1)} %reshape.295), channel_id=1, replica_groups=mesh['grid'=64,'comp'=8] {'comp'}, dimensions={0} | all-to-all | bytes 8192 | tf_op jit(solution)/shard_map/all_to_all | solution.py:50
  800.1 0.1 reshape.296
  800.2 0.1 reshape.282
  800.3 82.1 %all-gather = bf16[64,4,512]{2,1,0:T(4,128)(2,1)S(1)} all-gather(bf16[1,4,512]{2,1,0:T(4,128)(2,1)S(1)} %reshape.282), channel_id=1, replica_groups=mesh['grid'=64,'comp'=8] {'grid'}, dimensions={0}, use_global_device_ids=true | all-gather | bytes 266240 | tf_op jit(solution)/shard_map/all_gather | solution.py:51
  882.4 0.1 reshape.283
  882.5 0.0 all-gather.6.cloned.1.call-done
  882.5 3.3 fusion.36
  (3 shorter events, 0.0 us)
Async XLA Ops:
  6.5 253.1 %copy-start = (f32[1024,16]{0,1:T(8,128)S(1)}, f32[1024,16]{0,1:T(8,128)}, u32[]{:S(2)}) copy-start(f32[1024,16]{0,1:T(8,128)} %param.9) | copy-start | bytes 196612
  6.5 255.5 %copy-start.3 = (f32[8,64]{1,0:T(8,128)S(1)}, f32[8,64]{1,0:T(8,128)}, u32[]{:S(2)}) copy-start(f32[8,64]{1,0:T(8,128)} %param.12) | copy-start | bytes 6148
  6.5 255.5 %copy-start.2 = (f32[8,1024]{1,0:T(8,128)S(1)}, f32[8,1024]{1,0:T(8,128)}, u32[]{:S(2)}) copy-start(f32[8,1024]{1,0:T(8,128)} %param.10) | copy-start | bytes 98308
  6.5 255.6 %copy-start.1 = (f32[8,2048]{1,0:T(8,128)S(1)}, f32[8,2048]{1,0:T(8,128)}, u32[]{:S(2)}) copy-start(f32[8,2048]{1,0:T(8,128)} %param.11) | copy-start | bytes 196612
  6.5 104.4 %all-gather.4.cloned.1.call-start = ((), (), s32[]{:S(2)}) async-start(), calls=%async_computation.2 | async-start | bytes 4718592 | tf_op jit(solution)/shard_map/all_gather | solution.py:31
  7.3 765.8 %copy-start.4 = (f32[64]{0:T(128)S(1)}, f32[64]{0:T(128)}, u32[]{:S(2)}) copy-start(f32[64]{0:T(128)} %param.13) | copy-start | bytes 772
  7.3 252.3 %reduce-scatter.2.cloned.1.call-start = ((), (), s32[]{:S(2)}) async-start(), calls=%async_computation.3 | async-start | bytes 532480 | tf_op jit(solution)/shard_map/reduce_scatter | solution.py:37
  115.2 657.9 %all-reduce.2.cloned.1.call-start = ((), (), s32[]{:S(2)}) async-start(), calls=%async_computation.4 | async-start | bytes 524288 | tf_op jit(solution)/shard_map/psum | solution.py:41
  261.5 621.1 %all-gather.6.cloned.1.call-start = ((), (), s32[]{:S(2)}) async-start(), calls=%async_computation.5 | async-start | bytes 2359296 | tf_op jit(solution)/shard_map/all_gather | solution.py:55
Sparse Core Ops, SparseCore 0:
  9.5 101.4 all-gather.3
  115.5 144.1 reduce-scatter.1
  262.5 510.4 all-reduce.1
  775.2 54.9 all-gather.5
where the time goes:
time: 893 us; the launch traced here: 892 us
  waiting for transfers between devices  759 us (85%)
  blocking collectives  91.1 us (10%)
  matrix products  27.2 us (3%)
  between operations  13.3 us (1%)
    psum x1, waiting for transfers between devices, on_device(): alpha = lax.psum(alpha_part, 'grid')  509 us
    reduce_scatter x1, waiting for transfers between devices, on_device(): lax.psum_scatter(partial_coef, 'grid', scatter_dimension=0, tiled=True)  144 us
    all_gather x1, waiting for transfers between devices, on_device(): lax.all_gather(fields_runs, 'comp', axis=0, tiled=True)  104 us
    all_gather x1, blocking collectives, on_device(): pred_block = lax.all_gather(swapped, 'grid', axis=0, tiled=True)  82.1 us
    dot_general x1, matrix products, matern_block(): jnp.einsum('kni,ik->nk', cross, alpha, precision=lax.Precision.HIGHEST)  17.9 us
  transfers between devices with their start and end apart: 4, of which 3 were waited for; matrix products, arithmetic and copies ran while one was open for 2% of the time, Pallas kernels for 0%

commit v1 on v0

v1 whole, which is shorter than its diff:
```python
import math

import jax
import jax.numpy as jnp
from jax import lax
from jax.experimental import pallas as pl
from jax.experimental.pallas import tpu as pltpu
from jax.sharding import Mesh, PartitionSpec as P

GRID = ("zh", "y", "core")
COMP = ("x", "zl")
LOG2E = 1.4426950408889634
LN2 = 0.6931471805599453
F32 = jnp.float32
BF16 = jnp.bfloat16
HIGHEST = lax.Precision.HIGHEST
VMEM = pl.BlockSpec(memory_space=pltpu.VMEM)
SMEM = pl.BlockSpec(memory_space=pltpu.SMEM)


def params(mib):
    return pltpu.CompilerParams(vmem_limit_bytes=mib << 20)


def project_kernel(scale, own_ref, other_ref, basis_ref, out_ref):
    for half, runs_ref in enumerate((own_ref, other_ref)):
        part = lax.dot_general(
            basis_ref[...], runs_ref[...], (((1,), (1,)), ((), ())), preferred_element_type=F32
        )
        part = part * scale
        for block in range(4):
            out_ref[pl.ds(4 * half + block, 64, stride=8), :] = part[64 * block : 64 * block + 64]


def project(own, other, basis, scale):
    def body(*refs):
        project_kernel(scale, *refs)

    return pl.pallas_call(
        body,
        out_shape=jax.ShapeDtypeStruct((512, 128), F32),
        in_specs=[VMEM] * 3,
        out_specs=VMEM,
        compiler_params=params(16),
        cost_estimate=pl.CostEstimate(flops=1 << 28, bytes_accessed=1 << 21, transcendentals=0),
    )(own, other, basis)


def weights_kernel(place_ref, parts_ref, winv_ref, out_ref):
    coef = jnp.sum(parts_ref[...], axis=0)
    place = place_ref[0]
    own = jnp.dot(
        coef, winv_ref[pl.ds(pl.multiple_of(place * 128, 128), 128), :],
        precision=HIGHEST, preferred_element_type=F32,
    )
    other = jnp.dot(
        coef, winv_ref[pl.ds(pl.multiple_of((1 - place) * 128, 128), 128), :],
        precision=HIGHEST, preferred_element_type=F32,
    )
    row = lax.broadcasted_iota(jnp.int32, own.shape, 0)
    both = jnp.where(row < 4, own, other)
    for peer in range(4):
        out_ref[peer] = both


def weights(place, parts, winv):
    return pl.pallas_call(
        weights_kernel,
        out_shape=jax.ShapeDtypeStruct((4, 8, 1024), F32),
        in_specs=[SMEM, VMEM, VMEM],
        out_specs=VMEM,
        compiler_params=params(16),
        cost_estimate=pl.CostEstimate(flops=1 << 23, bytes_accessed=1 << 20, transcendentals=0),
    )(place, parts, winv)


def cross_kernel(var_ref, runs_ref, new_ref, out_ref):
    var = var_ref[pl.program_id(0)]
    for chunk in range(4):
        rows = slice(64 * chunk, 64 * chunk + 64)
        sq = jnp.dot(runs_ref[0, rows], new_ref[0], precision=HIGHEST, preferred_element_type=F32)
        sq = jnp.maximum(sq, 1e-30)
        dist = sq * lax.rsqrt(sq)
        out_ref[0, rows] = (var + (var * LN2) * dist) * jnp.exp2(-dist)


def cross_all(var, runs_feat, new_feat):
    return pl.pallas_call(
        cross_kernel,
        grid=(4, 4),
        out_shape=jax.ShapeDtypeStruct((4, 1024, 512), F32),
        in_specs=[
            SMEM,
            pl.BlockSpec((1, 256, 16), lambda b, i: (b, i, 0)),
            pl.BlockSpec((1, 16, 512), lambda b, i: (b, 0, 0)),
        ],
        out_specs=pl.BlockSpec((1, 256, 512), lambda b, i: (b, i, 0)),
        compiler_params=params(16),
        cost_estimate=pl.CostEstimate(
            flops=1 << 28, bytes_accessed=1 << 23, transcendentals=1 << 22
        ),
    )(var, runs_feat, new_feat)


def predict_kernel(cross_ref, pieces_ref, out_ref, spread_ref, pred_ref):
    block = pl.program_id(0)

    @pl.when(block == 0)
    def _():
        both = jnp.sum(pieces_ref[...], axis=0)
        first = both.astype(BF16)
        rest = both - first.astype(F32)
        second = rest.astype(BF16)
        third = (rest - second.astype(F32)).astype(BF16)
        lhs = jnp.concatenate([first.astype(F32), second.astype(F32), third.astype(F32)], axis=0)
        row = lax.broadcasted_iota(jnp.int32, (24, 512), 0)
        col = lax.broadcasted_iota(jnp.int32, (24, 512), 1)
        pick = (row % 4 == col // 128).astype(BF16)
        spread_ref[...] = jnp.dot(lhs.T.astype(BF16), pick, preferred_element_type=F32)

    def step(index, acc):
        base = pl.multiple_of(index * 64, 64)
        lanes = pl.ds(pl.multiple_of(block * 128, 128), 128)
        weight = spread_ref[pl.ds(base, 64), lanes]
        values = cross_ref[0, pl.ds(base, 64), :]
        sums = []
        for tile in range(4):
            prod = values[:, 128 * tile : 128 * tile + 128] * weight
            sums.append(jnp.sum(prod.reshape(8, 8, 128), axis=0))
        return tuple(a + s for a, s in zip(acc, sums))

    zero = jnp.zeros((8, 128), F32)
    acc = lax.fori_loop(0, 16, step, (zero,) * 4, unroll=2)
    for tile in range(4):
        where = (tile // 2) * 8 + 2 * block + tile % 2
        pred_ref[pl.ds(where, 1), :] = jnp.sum(acc[tile], axis=0, keepdims=True)

    @pl.when(block == 3)
    def _():
        tile = pred_ref[...].astype(BF16).reshape(1, 2, 8, 128)
        out_ref[...] = jnp.broadcast_to(tile, (64, 2, 8, 128))


def predict(cross, pieces):
    return pl.pallas_call(
        predict_kernel,
        grid=(4,),
        out_shape=jax.ShapeDtypeStruct((64, 2, 8, 128), BF16),
        in_specs=[
            pl.BlockSpec((1, 1024, 512), lambda b: (b, 0, 0)),
            pl.BlockSpec((4, 8, 1024), lambda b: (0, 0, 0)),
        ],
        out_specs=pl.BlockSpec((64, 2, 8, 128), lambda b: (0, 0, 0, 0)),
        scratch_shapes=[pltpu.VMEM((1024, 512), F32), pltpu.VMEM((16, 128), F32)],
        compiler_params=params(16),
        cost_estimate=pl.CostEstimate(flops=1 << 22, bytes_accessed=1 << 23, transcendentals=0),
    )(cross, pieces)


def rebuild_kernel(scale, place_ref, pred_ref, own_ref, other_ref, out_ref, wide_ref, lhs_ref):
    @pl.when(pl.program_id(0) == 0)
    def _():
        wide_ref[...] = pred_ref[...].astype(F32).reshape(1024, 128)
        place = place_ref[0]
        for side, which in enumerate((place, 1 - place)):
            rows = []
            for block in range(4):
                halves = [
                    wide_ref[pl.ds(8 * which + 2 * block + half, 64, stride=16), :]
                    for half in range(2)
                ]
                rows.append(jnp.concatenate(halves, axis=1))
            table = jnp.concatenate(rows, axis=0)
            lhs_ref[:, 256 * side : 256 * side + 256] = table.T.astype(BF16)

    total = jnp.dot(lhs_ref[:, :256], own_ref[...], preferred_element_type=F32)
    total = total + jnp.dot(lhs_ref[:, 256:], other_ref[...], preferred_element_type=F32)
    out_ref[...] = (total * scale).astype(BF16)


def rebuild(place, pred, own, other, scale):
    def body(*refs):
        rebuild_kernel(scale, *refs)

    width = 512
    return pl.pallas_call(
        body,
        grid=(2048 // width,),
        out_shape=jax.ShapeDtypeStruct((256, 2048), BF16),
        in_specs=[
            SMEM,
            pl.BlockSpec((64, 2, 8, 128), lambda i: (0, 0, 0, 0)),
            pl.BlockSpec((256, width), lambda i: (0, i)),
            pl.BlockSpec((256, width), lambda i: (0, i)),
        ],
        out_specs=pl.BlockSpec((256, width), lambda i: (0, i)),
        scratch_shapes=[pltpu.VMEM((1024, 128), F32), pltpu.VMEM((256, 512), BF16)],
        compiler_params=params(16),
        cost_estimate=pl.CostEstimate(flops=1 << 29, bytes_accessed=3 << 20, transcendentals=0),
    )(place, pred, own, other)


def kernel_params(lscale, variance, place, x):
    mine = jnp.concatenate([lscale, variance[None, :]], axis=0)
    mine = lax.dynamic_slice_in_dim(mine, place, 1, axis=1)
    mine = jnp.broadcast_to(jnp.pad(mine, ((0, 7), (0, 0))), (16, 128))
    by_shift = [mine]
    for shift in range(1, 4):
        by_shift.append(lax.ppermute(mine, "x", [(i, (i + shift) % 4) for i in range(4)]))
    stacked = jnp.stack([v[:9, 0] for v in by_shift])
    pick = (x - jnp.arange(4)) % 4
    chosen = jnp.sum(
        jnp.where(pick[:, None, None] == jnp.arange(4)[None, :, None], stacked[None], 0.0), axis=1
    )
    return chosen[:, :8], chosen[:, 8]


def features(lscale, design, new_settings, x):
    weight = (3.0 * LOG2E * LOG2E) / (lscale * lscale)
    new = lax.dynamic_slice_in_dim(new_settings, x * 512, 512, axis=1) - 0.5
    runs = design.T - 0.5
    ones_new = jnp.ones((4, 1, 512), F32)
    new_feat = jnp.concatenate(
        [
            -2.0 * weight[:, :, None] * new[None],
            ones_new,
            jnp.sum(weight[:, :, None] * (new * new)[None], axis=1, keepdims=True),
            jnp.zeros((4, 6, 512), F32),
        ],
        axis=1,
    )
    runs_feat = jnp.concatenate(
        [
            jnp.broadcast_to(runs[None], (4, 1024, 8)),
            jnp.sum((runs * runs)[None] * weight[:, None, :], axis=2, keepdims=True),
            jnp.ones((4, 1024, 1), F32),
            jnp.zeros((4, 1024, 6), F32),
        ],
        axis=2,
    )
    return runs_feat, new_feat


def on_device(fields_runs, eof_basis, weights_inv, design, new_settings, lscale, variance):
    x = lax.axis_index("x")
    place = lax.axis_index(GRID)
    zl = lax.axis_index("zl").reshape(1)
    swap = [(0, 1), (1, 0)]

    fields_other = lax.ppermute(fields_runs, "zl", swap)
    basis = lax.all_to_all(
        jnp.broadcast_to(eof_basis.T[None], (4, 64, 2048)), "x", 0, 0, tiled=True
    ).reshape(256, 2048)
    winv = lax.ppermute(
        weights_inv.T, ("zh", "x"), [(a * 4 + b, b * 4 + a) for a in range(4) for b in range(4)]
    )
    winv = lax.all_gather(winv, ("y", "core"), axis=0, tiled=True)

    scales, var = kernel_params(lscale, variance, place, x)
    runs_feat, new_feat = features(scales, design, new_settings, x)
    cross = cross_all(var, runs_feat, new_feat)

    partial = project(fields_runs, fields_other, basis, 1.0 / math.sqrt(131072))
    parts = lax.all_to_all(partial.reshape(64, 8, 128), GRID, 0, 0, tiled=True)
    basis_other = lax.ppermute(basis, "zl", swap)

    pieces = lax.all_to_all(weights(zl, parts, winv), "x", 0, 0, tiled=True)
    pred = predict(cross, pieces)
    pred = lax.all_to_all(pred.reshape(128, 8, 128), GRID + ("zl",), 0, 0, tiled=True)
    return rebuild(zl, pred.reshape(64, 2, 8, 128), basis, basis_other, 1.0 / math.sqrt(512))


def solution(mesh):
    fine = Mesh(mesh.devices.reshape(4, 8, 2, 4, 2), GRID + COMP)
    placed = (
        P(COMP, GRID),
        P(GRID, COMP),
        P(None, GRID),
        P(),
        P(),
        P(None, COMP),
        P(COMP),
    )
    return jax.shard_map(
        on_device, mesh=fine, in_specs=placed, out_specs=P(COMP, GRID), check_vma=False
    )
```

time: 893 us -> 155 us (0.17)
  waiting for transfers between devices: 759 us -> 43.1 us
  blocking collectives: 91.1 us -> 0 us
  starting transfers between devices: 0.15 us -> 60.6 us
  matrix products: 27.2 us -> 0 us
  Pallas kernels: 0 us -> 18.5 us
  local copies, waits for them, and re-layouts: 1.71 us -> 15.5 us
    psum x1 -> x0, waiting for transfers between devices: 509 us -> none  [on_device(): alpha = lax.psum(alpha_part, 'grid')]
    reduce_scatter x1 -> x0, waiting for transfers between devices: 144 us -> none  [on_device(): lax.psum_scatter(partial_coef, 'grid', scatter_dimension=0, tiled=True)]
    all_gather x2 -> x1, waiting for transfers between devices: 104 us -> 16.7 us  [on_device(): winv = lax.all_gather(winv, ('y', 'core'), axis=0, tiled=True)]
    all_gather x1 -> x0, blocking collectives: 82.1 us -> none  [on_device(): pred_block = lax.all_gather(swapped, 'grid', axis=0, tiled=True)]
    all_to_all x0 -> x4, starting transfers between devices: none -> 43.3 us  [the longest x1 23.9 us: on_device(): parts = lax.all_to_all(partial.reshape(64, 8, 128), GRID, 0, 0, tiled=True)]
    dot_general x4 -> x0, matrix products: 27.2 us -> none  [the longest x1 17.9 us: matern_block(): jnp.einsum('kni,ik->nk', cross, alpha, precision=lax.Precision.HIGHEST)]
    all_to_all x0 -> x4, waiting for transfers between devices: none -> 22 us  [the longest x1 14.8 us: on_device(): lax.all_to_all(pred.reshape(128, 8, 128), GRID + ('zl',), 0, 0, tiled=True)]
    pallas_call x0 -> x5, Pallas kernels: none -> 18.5 us  [the longest x1 10.1 us: cross_all(): pl.pallas_call(cross_kernel, grid=(4, 4), out_shape=jax.ShapeDtypeStruct(...]
  transfers between devices with their start and end apart: 4 -> 11, of which waited for: 3 -> 4; matrix products, arithmetic and copies ran while one was open for 2% -> 4% of each run, Pallas kernels for 0% -> 9%
where the time goes in v1:
time: 155 us; the launch traced here: 154 us
  starting transfers between devices  60.6 us (39%)
  waiting for transfers between devices  43.1 us (28%)
  Pallas kernels  18.5 us (12%)
  local copies, waits for them, and re-layouts  15.5 us (10%)
  between operations  13.7 us (9%)
  other arithmetic  2.79 us (2%)
    all_to_all x1, starting transfers between devices, on_device(): parts = lax.all_to_all(partial.reshape(64, 8, 128), GRID, 0, 0, tiled=True)  23.9 us
    all_gather x1, waiting for transfers between devices, on_device(): winv = lax.all_gather(winv, ('y', 'core'), axis=0, tiled=True)  16.7 us
    all_to_all x1, waiting for transfers between devices, on_device(): lax.all_to_all(pred.reshape(128, 8, 128), GRID + ('zl',), 0, 0, tiled=True)  14.8 us
    all_to_all x1, starting transfers between devices, on_device(): lax.all_to_all(pred.reshape(128, 8, 128), GRID + ('zl',), 0, 0, tiled=True)  12.4 us
    unnamed x18, local copies, waits for them, and re-layouts  10.6 us
    ppermute x3, starting transfers between devices, kernel_params(): lax.ppermute(mine, 'x', [(i, (i + shift) % 4) for i in range(4)])  10.2 us
    pallas_call x1, Pallas kernels, cross_all(): pl.pallas_call(cross_kernel, grid=(4, 4), out_shape=jax.ShapeDtypeStruct(...  10.1 us
    all_to_all x1, waiting for transfers between devices, on_device(): parts = lax.all_to_all(partial.reshape(64, 8, 128), GRID, 0, 0, tiled=True)  7.26 us
  transfers between devices with their start and end apart: 11, of which 4 were waited for; matrix products, arithmetic and copies ran while one was open for 4% of the time, Pallas kernels for 9%

profile of v1, /device:TPU:1, one launch (start us, length us, event | category | flops | bytes accessed | tf_op | source)
XLA Modules:
  0.0 154.1 jit_solution(5620227538605671084)
XLA Ops:
  6.5 0.9 fusion.3
  7.5 0.1 pad_reduce_fusion
  7.6 5.2 %collective-permute-start.2 = (f32[16,128]{0,1:T(8,128)S(1)}, f32[16,128]{0,1:T(8,128)S(1)}, u32[]{:S(2)}, u32[]{:S(2)}) collective-permute-start(f32[16,128]{0,1:T(8,128)S(1)} %broadcast_in_dim.72), channel_id=1, source_target_pairs={{0,6},{2,0},{4,2},{6,4},{1,7},{3,1},{5,3},{7,5},{8,14},{10,8},{12,... | collective-permute-start | bytes 24584 | tf_op jit(solution)/shard_map/ppermute | solution.py:209
  12.8 2.4 %collective-permute-start.1 = (f32[16,128]{0,1:T(8,128)S(1)}, f32[16,128]{0,1:T(8,128)S(1)}, u32[]{:S(2)}, u32[]{:S(2)}) collective-permute-start(f32[16,128]{0,1:T(8,128)S(1)} %broadcast_in_dim.72), channel_id=1, source_target_pairs={{0,4},{2,6},{4,0},{6,2},{1,5},{3,7},{5,1},{7,3},{8,12},{10,14},{12... | collective-permute-start | bytes 24584 | tf_op jit(solution)/shard_map/ppermute | solution.py:209
  15.3 2.5 %collective-permute-start = (f32[16,128]{0,1:T(8,128)S(1)}, f32[16,128]{0,1:T(8,128)S(1)}, u32[]{:S(2)}, u32[]{:S(2)}) collective-permute-start(f32[16,128]{0,1:T(8,128)S(1)} %broadcast_in_dim.72), channel_id=1, source_target_pairs={{0,2},{2,4},{4,6},{6,0},{1,3},{3,5},{5,7},{7,1},{8,10},{10,12},{12... | collective-permute-start | bytes 24584 | tf_op jit(solution)/shard_map/ppermute | solution.py:209
  17.8 2.0 %broadcast_in_dim.82 = bf16[4,64,2048]{2,1,0:T(8,128)(2,1)} broadcast(bf16[64,2048]{1,0:T(8,128)(2,1)} %bitcast.26), dimensions={1,2} | broadcast | bytes 1310720 | tf_op jit(solution)/shard_map/broadcast_in_dim | solution.py:252
  19.8 3.5 %all-to-all-start = ((bf16[4,64,2048]{2,1,0:T(8,128)(2,1)}), bf16[4,64,2048]{2,1,0:T(8,128)(2,1)S(1)}, u32[]{:S(2)}, u32[]{:S(2)}) async-start(bf16[4,64,2048]{2,1,0:T(8,128)(2,1)} %broadcast_in_dim.82), calls=%async_computation | async-start | bytes 2097152 | tf_op jit(solution)/shard_map/all_to_all | solution.py:251
  23.4 0.0 all-gather.2.cloned.1.call-start
  23.4 4.0 %collective-permute-start.3 = (bf16[128,2048]{1,0:T(8,128)(2,1)S(1)}, bf16[128,2048]{1,0:T(8,128)(2,1)S(1)}, u32[]{:S(2)}, u32[]{:S(2)}) collective-permute-start(bf16[128,2048]{1,0:T(8,128)(2,1)S(1)} %copy-done.3), channel_id=1, source_target_pairs={{0,1},{1,0},{2,3},{3,2},{4,5},{5,4},{6,7},{7,6},{8,9},{9,8},{10,11... | collective-permute-start | bytes 1572872 | tf_op jit(solution)/shard_map/ppermute | solution.py:250
  27.4 0.7 collective-permute-start.4
  28.2 0.1 iota_compare_fusion
  28.2 0.7 fusion.2
  29.0 0.1 pad.11.clone
  29.0 0.1 pad.6.clone
  29.1 0.1 pad.12.clone
  29.2 0.2 copy.27
  29.4 0.0 collective-permute-done.4
  29.4 0.6 copy-done.7
  30.0 0.0 all-gather.2.cloned.1.call-update
  30.1 0.0 collective-permute-done
  30.1 0.1 select_reduce_fusion
  30.2 0.1 multiply_reduce_fusion.1
  30.4 4.3 %collective-permute-done.3.refs_1_ = bf16[128,2048]{1,0:T(8,128)(2,1)S(1)} collective-permute-done((bf16[128,2048]{1,0:T(8,128)(2,1)S(1)}, bf16[128,2048]{1,0:T(8,128)(2,1)S(1)}, u32[]{:S(2)}, u32[]{:S(2)}) %collective-permute-start.3) | collective-permute-done | bytes 524320 | tf_op jit(solution)/shard_map/ppermute | solution.py:250
  34.7 0.0 all-to-all-done
  34.7 1.4 shard_map.74
  36.1 23.9 %all-to-all-start.1 = ((f32[64,8,128]{2,1,0:T(8,128)}), f32[64,8,128]{2,1,0:T(8,128)S(1)}, u32[]{:S(2)}, u32[]{:S(2)}) async-start(f32[64,8,128]{2,1,0:T(8,128)} %bitcast.9), calls=%async_computation.1 | async-start | bytes 524288 | tf_op jit(solution)/shard_map/all_to_all | solution.py:264
  60.0 0.1 maximum_maximum_fusion.1.new_ref
  60.1 2.4 %collective-permute-start.5 = (bf16[256,2048]{1,0:T(8,128)(2,1)S(1)}, bf16[256,2048]{1,0:T(8,128)(2,1)}, u32[]{:S(2)}, u32[]{:S(2)}) collective-permute-start(bf16[256,2048]{1,0:T(8,128)(2,1)S(1)} %bitcast.23), channel_id=1, source_target_pairs={{0,1},{1,0},{2,3},{3,2},{4,5},{5,4},{6,7},{7,6},{8,9},{9,8},{10,11... | collective-permute-start | bytes 3145736 | tf_op jit(solution)/shard_map/ppermute | solution.py:265
  62.5 0.1 multiply_reduce_fusion
  62.6 2.0 %copy.28 = f32[4,1024,1]{2,1,0:T(8,128)} copy(f32[4,1024,1]{1,0,2:T(4,128)S(1)} %bitcast.27) | data formatting | bytes 32768 | tf_op jit(solution)/shard_map/broadcast_in_dim | solution.py:235
  64.6 0.1 broadcast_in_dim.75
  64.7 1.4 copy-done.5
  66.2 0.6 maximum_maximum_fusion.runs_ref
  66.8 7.3 %all-to-all-done.1.parts_ref = f32[64,8,128]{2,1,0:T(8,128)S(1)} async-done(((f32[64,8,128]{2,1,0:T(8,128)}), f32[64,8,128]{2,1,0:T(8,128)S(1)}, u32[]{:S(2)}, u32[]{:S(2)}) %all-to-all-start.1) | async-done | bytes 262176 | tf_op jit(solution)/shard_map/all_to_all | solution.py:264
  74.1 16.7 %all-gather.2.cloned.1.call-done.winv_ref = f32[256,1024]{1,0:T(8,128)} async-done(((f32[16,1024]{1,0:T(8,128)}), f32[256,1024]{1,0:T(8,128)}) %all-gather.2.cloned.1.call-update) | async-done | bytes 1048592 | tf_op jit(solution)/shard_map/all_gather | solution.py:257
  90.7 1.2 copy-done.2
  92.0 0.6 shard_map.75
  92.6 0.7 copy-done.4
  93.2 3.5 %all-to-all-start.2 = ((f32[4,8,1024]{2,1,0:T(8,128)}), f32[4,8,1024]{2,1,0:T(8,128)S(1)}, u32[]{:S(2)}, u32[]{:S(2)}) async-start(f32[4,8,1024]{2,1,0:T(8,128)} %copy-done.4), calls=%async_computation.2 | async-start | bytes 262144 | tf_op jit(solution)/shard_map/all_to_all | solution.py:267
  96.8 0.2 slice_reduce_fusion.var_ref
  96.9 10.1 %shard_map.73.cross_ref = f32[4,1024,512]{2,1,0:T(8,128)S(1)} custom-call(f32[4]{0:T(128)S(1)} %slice_reduce_fusion.var_ref, f32[4,1024,16]{2,1,0:T(8,128)S(1)} %maximum_maximum_fusion.runs_ref, f32[4,16,512]{2,1,0:T(8,128)S(1)} %maximum_maximum_fusion.1.new_ref), custom_call_target="tpu_custom_call" | custom-call | flops 268435456 | bytes 8388608 | tf_op jit(solution)/shard_map/pallas_call | solution.py:88
  107.1 3.2 %copy-done = f32[4,1024,512]{2,1,0:T(8,128)} copy-done((f32[4,1024,512]{2,1,0:T(8,128)}, f32[4,1024,512]{2,1,0:T(8,128)S(1)}, u32[]{:S(2)}) %copy-start) | copy-done | bytes 8388632
  110.3 0.0 all-to-all-done.2.pieces_ref
  110.3 3.4 %copy-done.1 = f32[4,1024,512]{2,1,0:T(8,128)S(1)} copy-done((f32[4,1024,512]{2,1,0:T(8,128)S(1)}, f32[4,1024,512]{2,1,0:T(8,128)}, u32[]{:S(2)}) %copy-start.1) | copy-done | bytes 8388632
  113.7 2.2 %shard_map.76 = bf16[64,2,8,128]{3,2,1,0:T(8,128)(2,1)} custom-call(f32[4,1024,512]{2,1,0:T(8,128)S(1)} %copy-done.1, f32[4,8,1024]{2,1,0:T(8,128)S(1)} %all-to-all-done.2.pieces_ref), custom_call_target="tpu_custom_call" | custom-call | flops 4194304 | bytes 8388608 | tf_op jit(solution)/shard_map/pallas_call | solution.py:145
  115.9 12.4 %all-to-all-start.3 = ((bf16[128,8,128]{2,1,0:T(8,128)(2,1)}), bf16[128,8,128]{2,1,0:T(8,128)(2,1)S(1)}, u32[]{:S(2)}, u32[]{:S(2)}) async-start(bf16[128,8,128]{2,1,0:T(8,128)(2,1)} %bitcast.11), calls=%async_computation.3 | async-start | bytes 524288 | tf_op jit(solution)/shard_map/all_to_all | solution.py:269
  128.3 14.8 %all-to-all-done.3 = bf16[128,8,128]{2,1,0:T(8,128)(2,1)S(1)} async-done(((bf16[128,8,128]{2,1,0:T(8,128)(2,1)}), bf16[128,8,128]{2,1,0:T(8,128)(2,1)S(1)}, u32[]{:S(2)}, u32[]{:S(2)}) %all-to-all-start.3) | async-done | bytes 262176 | tf_op jit(solution)/shard_map/all_to_all | solution.py:269
  143.0 4.2 %shard_map.77 = bf16[256,2048]{1,0:T(8,128)(2,1)} custom-call(s32[1]{0:T(128)} %bitcast.place_ref.refs_0_, bf16[64,2,8,128]{3,2,1,0:T(8,128)(2,1)S(1)} %bitcast.25, bf16[256,2048]{1,0:T(8,128)(2,1)S(1)} %bitcast.24, bf16[256,2048]{1,0:T(8,128)(2,1)} %collective-permute-done.5.refs_3_), custom_call_target="tpu_custom_call" | custom-call | flops 536870912 | bytes 3145728 | tf_op jit(solution)/shard_map/pallas_call | solution.py:186
  (26 shorter events, 0.1 us)
Async XLA Ops:
  6.5 16.9 %copy-start.3 = (bf16[128,2048]{1,0:T(8,128)(2,1)S(1)}, bf16[128,2048]{1,0:T(8,128)(2,1)}, u32[]{:S(2)}) copy-start(bf16[128,2048]{1,0:T(8,128)(2,1)} %refs_0_.1) | copy-start | bytes 1572868
  6.5 20.9 %copy-start.8 = (f32[1024,16]{0,1:T(8,128)S(1)}, f32[1024,16]{0,1:T(8,128)}, u32[]{:S(2)}) copy-start(f32[1024,16]{0,1:T(8,128)} %param.9) | copy-start | bytes 196612
  6.5 21.6 %copy-start.6 = (f32[8,1024]{1,0:T(8,128)S(1)}, f32[8,1024]{1,0:T(8,128)}, u32[]{:S(2)}) copy-start(f32[8,1024]{1,0:T(8,128)} %param.10) | copy-start | bytes 98308
  7.6 22.4 %collective-permute-start.2 = (f32[16,128]{0,1:T(8,128)S(1)}, f32[16,128]{0,1:T(8,128)S(1)}, u32[]{:S(2)}, u32[]{:S(2)}) collective-permute-start(f32[16,128]{0,1:T(8,128)S(1)} %broadcast_in_dim.72), channel_id=1, source_target_pairs={{0,6},{2,0},{4,2},{6,4},{1,7},{3,1},{5,3},{7,5},{8,14},{10,8},{12,... | collective-permute-start | bytes 24584 | tf_op jit(solution)/shard_map/ppermute | solution.py:209
  12.8 17.2 %collective-permute-start.1 = (f32[16,128]{0,1:T(8,128)S(1)}, f32[16,128]{0,1:T(8,128)S(1)}, u32[]{:S(2)}, u32[]{:S(2)}) collective-permute-start(f32[16,128]{0,1:T(8,128)S(1)} %broadcast_in_dim.72), channel_id=1, source_target_pairs={{0,4},{2,6},{4,0},{6,2},{1,5},{3,7},{5,1},{7,3},{8,12},{10,14},{12... | collective-permute-start | bytes 24584 | tf_op jit(solution)/shard_map/ppermute | solution.py:209
  15.3 14.8 %collective-permute-start = (f32[16,128]{0,1:T(8,128)S(1)}, f32[16,128]{0,1:T(8,128)S(1)}, u32[]{:S(2)}, u32[]{:S(2)}) collective-permute-start(f32[16,128]{0,1:T(8,128)S(1)} %broadcast_in_dim.72), channel_id=1, source_target_pairs={{0,2},{2,4},{4,6},{6,0},{1,3},{3,5},{5,7},{7,1},{8,10},{10,12},{12... | collective-permute-start | bytes 24584 | tf_op jit(solution)/shard_map/ppermute | solution.py:209
  19.8 14.9 %all-to-all-start = ((bf16[4,64,2048]{2,1,0:T(8,128)(2,1)}), bf16[4,64,2048]{2,1,0:T(8,128)(2,1)S(1)}, u32[]{:S(2)}, u32[]{:S(2)}) async-start(bf16[4,64,2048]{2,1,0:T(8,128)(2,1)} %broadcast_in_dim.82), calls=%async_computation | async-start | bytes 2097152 | tf_op jit(solution)/shard_map/all_to_all | solution.py:251
  23.4 67.4 %all-gather.2.cloned.1.call-start = ((), (), s32[]{:S(2)}) async-start(), calls=%async_computation.4 | async-start | bytes 1114112 | tf_op jit(solution)/shard_map/all_gather | solution.py:257
  23.4 11.3 %collective-permute-start.3 = (bf16[128,2048]{1,0:T(8,128)(2,1)S(1)}, bf16[128,2048]{1,0:T(8,128)(2,1)S(1)}, u32[]{:S(2)}, u32[]{:S(2)}) collective-permute-start(bf16[128,2048]{1,0:T(8,128)(2,1)S(1)} %copy-done.3), channel_id=1, source_target_pairs={{0,1},{1,0},{2,3},{3,2},{4,5},{5,4},{6,7},{7,6},{8,9},{9,8},{10,11... | collective-permute-start | bytes 1572872 | tf_op jit(solution)/shard_map/ppermute | solution.py:250
  27.4 2.0 %collective-permute-start.4 = (f32[16,1024]{1,0:T(8,128)S(1)}, f32[16,1024]{1,0:T(8,128)S(1)}, u32[]{:S(2)}, u32[]{:S(2)}) collective-permute-start(f32[16,1024]{1,0:T(8,128)S(1)} %bitcast.30), channel_id=1, source_target_pairs={{0,0},{2,128},{4,256},{6,384},{128,2},{130,130},{132,258},{134,386... | collective-permute-start | bytes 196616 | tf_op jit(solution)/shard_map/ppermute | solution.py:254
  29.4 0.6 copy-start.7
  36.1 38.0 %all-to-all-start.1 = ((f32[64,8,128]{2,1,0:T(8,128)}), f32[64,8,128]{2,1,0:T(8,128)S(1)}, u32[]{:S(2)}, u32[]{:S(2)}) async-start(f32[64,8,128]{2,1,0:T(8,128)} %bitcast.9), calls=%async_computation.1 | async-start | bytes 524288 | tf_op jit(solution)/shard_map/all_to_all | solution.py:264
  60.1 68.2 %collective-permute-start.5 = (bf16[256,2048]{1,0:T(8,128)(2,1)S(1)}, bf16[256,2048]{1,0:T(8,128)(2,1)}, u32[]{:S(2)}, u32[]{:S(2)}) collective-permute-start(bf16[256,2048]{1,0:T(8,128)(2,1)S(1)} %bitcast.23), channel_id=1, source_target_pairs={{0,1},{1,0},{2,3},{3,2},{4,5},{5,4},{6,7},{7,6},{8,9},{9,8},{10,11... | collective-permute-start | bytes 3145736 | tf_op jit(solution)/shard_map/ppermute | solution.py:265
  64.6 1.6 %copy-start.5 = (f32[4,1024,1]{2,1,0:T(8,128)S(1)}, f32[4,1024,1]{2,1,0:T(8,128)}, u32[]{:S(2)}) copy-start(f32[4,1024,1]{2,1,0:T(8,128)} %copy.28) | copy-start | bytes 49156
  90.7 1.2 copy-start.2
  92.6 0.7 copy-start.4
  93.2 17.1 %all-to-all-start.2 = ((f32[4,8,1024]{2,1,0:T(8,128)}), f32[4,8,1024]{2,1,0:T(8,128)S(1)}, u32[]{:S(2)}, u32[]{:S(2)}) async-start(f32[4,8,1024]{2,1,0:T(8,128)} %copy-done.4), calls=%async_computation.2 | async-start | bytes 262144 | tf_op jit(solution)/shard_map/all_to_all | solution.py:267
  107.1 3.2 %copy-start = (f32[4,1024,512]{2,1,0:T(8,128)}, f32[4,1024,512]{2,1,0:T(8,128)S(1)}, u32[]{:S(2)}) copy-start(f32[4,1024,512]{2,1,0:T(8,128)S(1)} %shard_map.73.cross_ref) | copy-start | bytes 25165828
  110.3 3.4 %copy-start.1 = (f32[4,1024,512]{2,1,0:T(8,128)S(1)}, f32[4,1024,512]{2,1,0:T(8,128)}, u32[]{:S(2)}) copy-start(f32[4,1024,512]{2,1,0:T(8,128)} %copy-done) | copy-start | bytes 25165828
  115.9 27.2 %all-to-all-start.3 = ((bf16[128,8,128]{2,1,0:T(8,128)(2,1)}), bf16[128,8,128]{2,1,0:T(8,128)(2,1)S(1)}, u32[]{:S(2)}, u32[]{:S(2)}) async-start(bf16[128,8,128]{2,1,0:T(8,128)(2,1)} %bitcast.11), calls=%async_computation.3 | async-start | bytes 524288 | tf_op jit(solution)/shard_map/all_to_all | solution.py:269
Sparse Core Ops, SparseCore 0:
  30.2 60.5 all-gather.1

commit v2 on v1

--- a/solution.py
+++ b/solution.py
@@ -16,16 +16,50 @@
 HIGHEST = lax.Precision.HIGHEST
 VMEM = pl.BlockSpec(memory_space=pltpu.VMEM)
 SMEM = pl.BlockSpec(memory_space=pltpu.SMEM)
+CELLS = 2048
+WIDE = CELLS + 128
 
 
 def params(mib):
     return pltpu.CompilerParams(vmem_limit_bytes=mib << 20)
+
+
+def split3(value):
+    first = value.astype(BF16)
+    rest = value - first.astype(F32)
+    second = rest.astype(BF16)
+    third = (rest - second.astype(F32)).astype(BF16)
+    return first, second, third
+
+
+def pack_kernel(basis_ref, lscale_ref, variance_ref, out_ref):
+    row = lax.broadcasted_iota(jnp.int32, (8, 64), 0)
+    tail = jnp.where(row == 0, jnp.broadcast_to(variance_ref[...], (8, 64)), 0.0)
+    value = jnp.concatenate([lscale_ref[...], tail], axis=0)
+    pieces = jnp.concatenate([part.astype(F32) for part in split3(value)], axis=0)
+    pieces = jnp.concatenate([pieces, jnp.zeros((80, 64), F32)], axis=0)
+    side = jnp.concatenate([pieces, jnp.zeros((128, 64), F32)], axis=1).T[:64].astype(BF16)
+    basis = basis_ref[...]
+    for peer in range(4):
+        out_ref[peer, :, :CELLS] = basis
+        out_ref[peer, :, CELLS:] = side
+
+
+def pack(basis, lscale, variance):
+    return pl.pallas_call(
+        pack_kernel,
+        out_shape=jax.ShapeDtypeStruct((4, 64, WIDE), BF16),
+        in_specs=[VMEM] * 3,
+        out_specs=VMEM,
+        compiler_params=params(16),
+        cost_estimate=pl.CostEstimate(flops=0, bytes_accessed=5 << 18, transcendentals=0),
+    )(basis, lscale, variance)
 
 
 def project_kernel(scale, own_ref, other_ref, basis_ref, out_ref):
     for half, runs_ref in enumerate((own_ref, other_ref)):
         part = lax.dot_general(
-            basis_ref[...], runs_ref[...], (((1,), (1,)), ((), ())), preferred_element_type=F32
+            basis_ref[:, :CELLS], runs_ref[...], (((1,), (1,)), ((), ())), preferred_element_type=F32
         )
         part = part * scale
         for block in range(4):
@@ -46,7 +80,7 @@
     )(own, other, basis)
 
 
-def weights_kernel(place_ref, parts_ref, winv_ref, out_ref):
+def weights_kernel(place_ref, parts_ref, winv_ref, after_ref, out_ref):
     coef = jnp.sum(parts_ref[...], axis=0)
     place = place_ref[0]
     own = jnp.dot(
@@ -63,56 +97,87 @@
         out_ref[peer] = both
 
 
-def weights(place, parts, winv):
+def weights(place, parts, winv, after):
     return pl.pallas_call(
         weights_kernel,
         out_shape=jax.ShapeDtypeStruct((4, 8, 1024), F32),
-        in_specs=[SMEM, VMEM, VMEM],
+        in_specs=[SMEM, VMEM, VMEM, pl.BlockSpec(memory_space=pl.ANY)],
         out_specs=VMEM,
         compiler_params=params(16),
         cost_estimate=pl.CostEstimate(flops=1 << 23, bytes_accessed=1 << 20, transcendentals=0),
-    )(place, parts, winv)
-
-
-def cross_kernel(var_ref, runs_ref, new_ref, out_ref):
-    var = var_ref[pl.program_id(0)]
-    for chunk in range(4):
+    )(place, parts, winv, after)
+
+
+def cross_kernel(where_ref, side_ref, design_ref, new_ref, out_ref, aux_ref, side_wide, runs_feat):
+    block = pl.program_id(0)
+
+    @pl.when(block == 0)
+    def _():
+        side_wide[...] = side_ref[...].astype(F32)
+        runs = design_ref[...] - 0.5
+        first, second, third = split3(jnp.concatenate([runs, runs * runs], axis=0))
+        row = lax.broadcasted_iota(jnp.int32, (32, 1024), 0)
+        ones = jnp.where(row < 3, 1.0, 0.0)
+        parts = [first, first, first, second, second, third]
+        table = jnp.concatenate([p.astype(F32) for p in parts] + [ones], axis=0)
+        runs_feat[...] = table.T.astype(BF16)
+
+    mine = side_wide[pl.ds(64 * block + where_ref[1], 1), :]
+    column = jnp.broadcast_to(mine, (128, 128)).T
+    value = (column[0:16] + column[16:32]) + column[32:48]
+    aux_ref[pl.ds(block, 1), :] = value[8:9] * LN2
+    lscale = value[:8]
+    weight = (3.0 * LOG2E * LOG2E) / (lscale * lscale)
+    weight = jnp.concatenate([weight] * 4, axis=1)
+    new = new_ref[:, pl.ds(pl.multiple_of(where_ref[0] * 512, 512), 512)] - 0.5
+    scaled = weight * new
+    first, second, third = split3(jnp.concatenate([-2.0 * scaled, weight], axis=0))
+    square = jnp.broadcast_to(jnp.sum(scaled * new, axis=0, keepdims=True), (32, 512))
+    row = lax.broadcasted_iota(jnp.int32, (32, 512), 0)
+    lead, mid, low = [p.astype(F32) for p in split3(square)]
+    tail = jnp.where(row == 0, lead, jnp.where(row == 1, mid, jnp.where(row == 2, low, 0.0)))
+    rhs = jnp.concatenate([first, second, third, first, second, first, tail.astype(BF16)], axis=0)
+    for chunk in range(16):
         rows = slice(64 * chunk, 64 * chunk + 64)
-        sq = jnp.dot(runs_ref[0, rows], new_ref[0], precision=HIGHEST, preferred_element_type=F32)
+        sq = jnp.dot(runs_feat[rows], rhs, preferred_element_type=F32)
         sq = jnp.maximum(sq, 1e-30)
         dist = sq * lax.rsqrt(sq)
-        out_ref[0, rows] = (var + (var * LN2) * dist) * jnp.exp2(-dist)
-
-
-def cross_all(var, runs_feat, new_feat):
+        out_ref[0, rows] = (LOG2E + dist) * jnp.exp2(-dist)
+
+
+def cross_all(where, basis, design, new_settings):
     return pl.pallas_call(
         cross_kernel,
-        grid=(4, 4),
-        out_shape=jax.ShapeDtypeStruct((4, 1024, 512), F32),
+        grid=(4,),
+        out_shape=(
+            jax.ShapeDtypeStruct((4, 1024, 512), F32),
+            jax.ShapeDtypeStruct((8, 128), F32),
+        ),
         in_specs=[
             SMEM,
-            pl.BlockSpec((1, 256, 16), lambda b, i: (b, i, 0)),
-            pl.BlockSpec((1, 16, 512), lambda b, i: (b, 0, 0)),
+            pl.BlockSpec((256, 128), lambda b: (0, CELLS // 128)),
+            pl.BlockSpec((8, 1024), lambda b: (0, 0)),
+            pl.BlockSpec((8, 2048), lambda b: (0, 0)),
         ],
-        out_specs=pl.BlockSpec((1, 256, 512), lambda b, i: (b, i, 0)),
+        out_specs=(
+            pl.BlockSpec((1, 1024, 512), lambda b: (b, 0, 0)),
+            pl.BlockSpec((8, 128), lambda b: (0, 0)),
+        ),
+        scratch_shapes=[pltpu.VMEM((256, 128), F32), pltpu.VMEM((1024, 128), BF16)],
         compiler_params=params(16),
         cost_estimate=pl.CostEstimate(
             flops=1 << 28, bytes_accessed=1 << 23, transcendentals=1 << 22
         ),
-    )(var, runs_feat, new_feat)
-
-
-def predict_kernel(cross_ref, pieces_ref, out_ref, spread_ref, pred_ref):
+    )(where, basis, design, new_settings)
+
+
+def predict_kernel(cross_ref, pieces_ref, aux_ref, out_ref, spread_ref, pred_ref):
     block = pl.program_id(0)
 
     @pl.when(block == 0)
     def _():
         both = jnp.sum(pieces_ref[...], axis=0)
-        first = both.astype(BF16)
-        rest = both - first.astype(F32)
-        second = rest.astype(BF16)
-        third = (rest - second.astype(F32)).astype(BF16)
-        lhs = jnp.concatenate([first.astype(F32), second.astype(F32), third.astype(F32)], axis=0)
+        lhs = jnp.concatenate([p.astype(F32) for p in split3(both)], axis=0)
         row = lax.broadcasted_iota(jnp.int32, (24, 512), 0)
         col = lax.broadcasted_iota(jnp.int32, (24, 512), 1)
         pick = (row % 4 == col // 128).astype(BF16)
@@ -133,7 +198,8 @@
     acc = lax.fori_loop(0, 16, step, (zero,) * 4, unroll=2)
     for tile in range(4):
         where = (tile // 2) * 8 + 2 * block + tile % 2
-        pred_ref[pl.ds(where, 1), :] = jnp.sum(acc[tile], axis=0, keepdims=True)
+        total = jnp.sum(acc[tile], axis=0, keepdims=True)
+        pred_ref[pl.ds(where, 1), :] = total * aux_ref[pl.ds(block, 1), :]
 
     @pl.when(block == 3)
     def _():
@@ -141,7 +207,7 @@
         out_ref[...] = jnp.broadcast_to(tile, (64, 2, 8, 128))
 
 
-def predict(cross, pieces):
+def predict(cross, pieces, aux):
     return pl.pallas_call(
         predict_kernel,
         grid=(4,),
@@ -149,12 +215,13 @@
         in_specs=[
             pl.BlockSpec((1, 1024, 512), lambda b: (b, 0, 0)),
             pl.BlockSpec((4, 8, 1024), lambda b: (0, 0, 0)),
+            pl.BlockSpec((8, 128), lambda b: (0, 0)),
         ],
         out_specs=pl.BlockSpec((64, 2, 8, 128), lambda b: (0, 0, 0, 0)),
         scratch_shapes=[pltpu.VMEM((1024, 512), F32), pltpu.VMEM((16, 128), F32)],
         compiler_params=params(16),
         cost_estimate=pl.CostEstimate(flops=1 << 22, bytes_accessed=1 << 23, transcendentals=0),
-    )(cross, pieces)
+    )(cross, pieces, aux)
 
 
 def rebuild_kernel(scale, place_ref, pred_ref, own_ref, other_ref, out_ref, wide_ref, lhs_ref):
@@ -200,72 +267,32 @@
     )(place, pred, own, other)
 
 
-def kernel_params(lscale, variance, place, x):
-    mine = jnp.concatenate([lscale, variance[None, :]], axis=0)
-    mine = lax.dynamic_slice_in_dim(mine, place, 1, axis=1)
-    mine = jnp.broadcast_to(jnp.pad(mine, ((0, 7), (0, 0))), (16, 128))
-    by_shift = [mine]
-    for shift in range(1, 4):
-        by_shift.append(lax.ppermute(mine, "x", [(i, (i + shift) % 4) for i in range(4)]))
-    stacked = jnp.stack([v[:9, 0] for v in by_shift])
-    pick = (x - jnp.arange(4)) % 4
-    chosen = jnp.sum(
-        jnp.where(pick[:, None, None] == jnp.arange(4)[None, :, None], stacked[None], 0.0), axis=1
-    )
-    return chosen[:, :8], chosen[:, 8]
-
-
-def features(lscale, design, new_settings, x):
-    weight = (3.0 * LOG2E * LOG2E) / (lscale * lscale)
-    new = lax.dynamic_slice_in_dim(new_settings, x * 512, 512, axis=1) - 0.5
-    runs = design.T - 0.5
-    ones_new = jnp.ones((4, 1, 512), F32)
-    new_feat = jnp.concatenate(
-        [
-            -2.0 * weight[:, :, None] * new[None],
-            ones_new,
-            jnp.sum(weight[:, :, None] * (new * new)[None], axis=1, keepdims=True),
-            jnp.zeros((4, 6, 512), F32),
-        ],
-        axis=1,
-    )
-    runs_feat = jnp.concatenate(
-        [
-            jnp.broadcast_to(runs[None], (4, 1024, 8)),
-            jnp.sum((runs * runs)[None] * weight[:, None, :], axis=2, keepdims=True),
-            jnp.ones((4, 1024, 1), F32),
-            jnp.zeros((4, 1024, 6), F32),
-        ],
-        axis=2,
-    )
-    return runs_feat, new_feat
-
-
 def on_device(fields_runs, eof_basis, weights_inv, design, new_settings, lscale, variance):
     x = lax.axis_index("x")
-    place = lax.axis_index(GRID)
     zl = lax.axis_index("zl").reshape(1)
+    where = jnp.stack([x, lax.axis_index(GRID)])
     swap = [(0, 1), (1, 0)]
+    own = eof_basis.T
 
     fields_other = lax.ppermute(fields_runs, "zl", swap)
     basis = lax.all_to_all(
-        jnp.broadcast_to(eof_basis.T[None], (4, 64, 2048)), "x", 0, 0, tiled=True
-    ).reshape(256, 2048)
+        pack(own, lscale, variance.reshape(1, 64)), "x", 0, 0, tiled=True
+    ).reshape(256, WIDE)
     winv = lax.ppermute(
         weights_inv.T, ("zh", "x"), [(a * 4 + b, b * 4 + a) for a in range(4) for b in range(4)]
     )
-    winv = lax.all_gather(winv, ("y", "core"), axis=0, tiled=True)
-
-    scales, var = kernel_params(lscale, variance, place, x)
-    runs_feat, new_feat = features(scales, design, new_settings, x)
-    cross = cross_all(var, runs_feat, new_feat)
+    winv = lax.all_gather(winv, "core", axis=0, tiled=True)
+    winv = lax.all_gather(winv, "y", axis=0, tiled=True)
 
     partial = project(fields_runs, fields_other, basis, 1.0 / math.sqrt(131072))
     parts = lax.all_to_all(partial.reshape(64, 8, 128), GRID, 0, 0, tiled=True)
-    basis_other = lax.ppermute(basis, "zl", swap)
-
-    pieces = lax.all_to_all(weights(zl, parts, winv), "x", 0, 0, tiled=True)
-    pred = predict(cross, pieces)
+
+    cross, aux = cross_all(where, basis, design, new_settings)
+    own, _ = lax.optimization_barrier((own, partial))
+    basis_other = lax.all_gather(lax.ppermute(own, "zl", swap), "x", axis=0, tiled=True)
+
+    pieces = lax.all_to_all(weights(zl, parts, winv, aux), "x", 0, 0, tiled=True)
+    pred = predict(cross, pieces, aux)
     pred = lax.all_to_all(pred.reshape(128, 8, 128), GRID + ("zl",), 0, 0, tiled=True)
     return rebuild(zl, pred.reshape(64, 2, 8, 128), basis, basis_other, 1.0 / math.sqrt(512))
 

time: 155 us -> 139 us (0.90)
  blocking collectives: 0 us -> 41.4 us
  starting transfers between devices: 60.6 us -> 36.2 us
  waiting for transfers between devices: 43.1 us -> 23.4 us
  Pallas kernels: 18.5 us -> 11.5 us
  local copies, waits for them, and re-layouts: 15.5 us -> 12.1 us
  other arithmetic: 2.79 us -> 0.08 us
    all_to_all x0 -> x2, blocking collectives: none -> 32.9 us  [the longest x1 24.7 us: on_device(): lax.all_to_all(pred.reshape(128, 8, 128), GRID + ('zl',), 0, 0, tiled=True)]
    all_gather x1 -> x2, waiting for transfers between devices: 16.7 us -> 0.01 us  [the longest x1 0.01 us: on_device(): winv = lax.all_gather(winv, 'y', axis=0, tiled=True)]
    all_to_all x3 -> x1, waiting for transfers between devices: 14.8 us -> 0.01 us  [on_device(): lax.all_to_all(pack(own, lscale, variance.reshape(1, 64)), 'x', 0, 0, til...]
    ppermute x4 -> x1, starting transfers between devices: 12.6 us -> 3.43 us  [on_device(): lax.ppermute(own, 'zl', swap)]
    all_to_all x1, starting transfers between devices: 23.9 us -> 15.2 us  [on_device(): parts = lax.all_to_all(partial.reshape(64, 8, 128), GRID, 0, 0, tiled=True)]
    all_gather x0 -> x1, blocking collectives: none -> 8.55 us  [on_device(): winv = lax.all_gather(winv, 'core', axis=0, tiled=True)]
    all_to_all x3 -> x1, starting transfers between devices: 19.4 us -> 11.6 us  [on_device(): lax.all_to_all(pack(own, lscale, variance.reshape(1, 64)), 'x', 0, 0, til...]
    ppermute x1, waiting for transfers between devices: 4.33 us -> 11.8 us  [on_device(): fields_other = lax.ppermute(fields_runs, 'zl', swap)]
  transfers between devices with their start and end apart: 11 -> 7, of which waited for: 4 -> 3; matrix products, arithmetic and copies ran while one was open for 4% -> 0% of each run, Pallas kernels for 9% -> 6%
where the time goes in v2:
time: 139 us; the launch traced here: 138 us
  blocking collectives  41.4 us (30%)
  starting transfers between devices  36.2 us (26%)
  waiting for transfers between devices  23.4 us (17%)
  between operations  13.5 us (10%)
  local copies, waits for them, and re-layouts  12.1 us (9%)
  Pallas kernels  11.5 us (8%)
    all_to_all x1, blocking collectives, on_device(): lax.all_to_all(pred.reshape(128, 8, 128), GRID + ('zl',), 0, 0, tiled=True)  24.7 us
    all_to_all x1, starting transfers between devices, on_device(): parts = lax.all_to_all(partial.reshape(64, 8, 128), GRID, 0, 0, tiled=True)  15.2 us
    unnamed x24, local copies, waits for them, and re-layouts  12.1 us
    ppermute x1, waiting for transfers between devices, on_device(): fields_other = lax.ppermute(fields_runs, 'zl', swap)  11.8 us
    all_to_all x1, starting transfers between devices, on_device(): lax.all_to_all(pack(own, lscale, variance.reshape(1, 64)), 'x', 0, 0, til...  11.6 us
    all_gather x1, blocking collectives, on_device(): winv = lax.all_gather(winv, 'core', axis=0, tiled=True)  8.55 us
    all_to_all x1, blocking collectives, on_device(): lax.all_to_all(weights(zl, parts, winv, aux), 'x', 0, 0, tiled=True)  8.15 us
    all_to_all x1, waiting for transfers between devices, on_device(): parts = lax.all_to_all(partial.reshape(64, 8, 128), GRID, 0, 0, tiled=True)  6.34 us
  transfers between devices with their start and end apart: 7, of which 3 were waited for; matrix products, arithmetic and copies ran while one was open for 0% of the time, Pallas kernels for 6%

profile of v2, /device:TPU:1, one launch (start us, length us, event | category | flops | bytes accessed | tf_op | source)
XLA Modules:
  0.0 138.2 jit_solution(12257665956776566765)
XLA Ops:
  6.5 0.0 all-gather.3.cloned.1.call-start
  6.5 1.5 %collective-permute-start.1 = (f32[16,1024]{1,0:T(8,128)}, f32[16,1024]{1,0:T(8,128)S(1)}, u32[]{:S(2)}, u32[]{:S(2)}) collective-permute-start(f32[16,1024]{1,0:T(8,128)} %bitcast.18), channel_id=1, source_target_pairs={{0,0},{2,128},{4,256},{6,384},{128,2},{130,130},{132,258},{134,386... | collective-permute-start | bytes 196616 | tf_op jit(solution)/shard_map/ppermute | solution.py:281
  8.0 0.0 collective-permute-done.1
  8.0 8.5 %all_gather.9 = f32[32,1024]{1,0:T(8,128)} all-gather(f32[16,1024]{1,0:T(8,128)S(1)} %collective-permute-done.1), channel_id=1, replica_groups=mesh['zh'=4,'y'=8,'core'=2,'x'=4,'zl'=2] {'core'}, dimensions={0}, use_global_device_ids=true | all-gather | bytes 196608 | tf_op jit(solution)/shard_map/all_gather | solution.py:284
  16.6 0.0 all-gather.3.cloned.1.call-update
  16.6 0.0 copy-start.5
  16.6 0.9 copy-done.5
  17.6 0.0 copy-start.7
  17.6 0.7 copy-done.7
  18.2 0.0 copy-start.8
  18.2 0.7 copy-done.8
  18.9 1.1 shard_map.73
  20.0 0.0 copy-start.4
  20.0 11.6 %all-to-all-start = ((bf16[4,64,2176]{2,1,0:T(8,128)(2,1)}), bf16[4,64,2176]{2,1,0:T(8,128)(2,1)S(1)}, u32[]{:S(2)}, u32[]{:S(2)}) async-start(bf16[4,64,2176]{2,1,0:T(8,128)(2,1)} %shard_map.73), calls=%async_computation | async-start | bytes 2228224 | tf_op jit(solution)/shard_map/all_to_all | solution.py:278
  31.6 0.0 all-gather.5.cloned.1.call-start
  31.6 0.0 copy-done.4
  31.6 4.4 %collective-permute-start = (bf16[128,2048]{1,0:T(8,128)(2,1)S(1)}, bf16[128,2048]{1,0:T(8,128)(2,1)S(1)}, u32[]{:S(2)}, u32[]{:S(2)}) collective-permute-start(bf16[128,2048]{1,0:T(8,128)(2,1)S(1)} %copy-done.4), channel_id=1, source_target_pairs={{0,1},{1,0},{2,3},{3,2},{4,5},{5,4},{6,7},{7,6},{8,9},{9,8},{10,11... | collective-permute-start | bytes 1572872 | tf_op jit(solution)/shard_map/ppermute | solution.py:277
  36.0 11.8 %collective-permute-done.refs_1_ = bf16[128,2048]{1,0:T(8,128)(2,1)S(1)} collective-permute-done((bf16[128,2048]{1,0:T(8,128)(2,1)S(1)}, bf16[128,2048]{1,0:T(8,128)(2,1)S(1)}, u32[]{:S(2)}, u32[]{:S(2)}) %collective-permute-start) | collective-permute-done | bytes 524320 | tf_op jit(solution)/shard_map/ppermute | solution.py:277
  47.8 0.0 all-to-all-done
  47.8 0.0 copy-start.6
  47.8 0.0 copy-start.9
  47.8 0.0 copy-start.10
  47.8 1.4 %shard_map.75 = f32[512,128]{1,0:T(8,128)} custom-call(bf16[128,2048]{1,0:T(8,128)(2,1)S(1)} %copy-done.4, bf16[128,2048]{1,0:T(8,128)(2,1)S(1)} %collective-permute-done.refs_1_, bf16[256,2176]{1,0:T(8,128)(2,1)S(1)} %bitcast.10), custom_call_target="tpu_custom_call" | custom-call | flops 268435456 | bytes 2097152 | tf_op jit(solution)/shard_map/pallas_call | solution.py:73
  49.3 0.0 copy-done.6
  49.3 3.4 %collective-permute-start.2 = (bf16[64,2048]{1,0:T(8,128)(2,1)S(1)}, bf16[64,2048]{1,0:T(8,128)(2,1)S(1)}, u32[]{:S(2)}, u32[]{:S(2)}) collective-permute-start(bf16[64,2048]{1,0:T(8,128)(2,1)S(1)} %bitcast.16), channel_id=1, source_target_pairs={{0,1},{1,0},{2,3},{3,2},{4,5},{5,4},{6,7},{7,6},{8,9},{9,8},{10,11... | collective-permute-start | bytes 786440 | tf_op jit(solution)/shard_map/ppermute | solution.py:292
  52.7 5.2 %collective-permute-done.2 = bf16[64,2048]{1,0:T(8,128)(2,1)S(1)} collective-permute-done((bf16[64,2048]{1,0:T(8,128)(2,1)S(1)}, bf16[64,2048]{1,0:T(8,128)(2,1)S(1)}, u32[]{:S(2)}, u32[]{:S(2)}) %collective-permute-start.2) | collective-permute-done | bytes 262176 | tf_op jit(solution)/shard_map/ppermute | solution.py:292
  57.9 0.0 copy-start.11
  57.9 0.7 copy-done.11
  58.6 0.0 all-gather.5.cloned.1.call-update
  58.6 15.2 %all-to-all-start.1 = ((f32[64,8,128]{2,1,0:T(8,128)}), f32[64,8,128]{2,1,0:T(8,128)S(1)}, u32[]{:S(2)}, u32[]{:S(2)}) async-start(f32[64,8,128]{2,1,0:T(8,128)} %bitcast.6), calls=%async_computation.1 | async-start | bytes 524288 | tf_op jit(solution)/shard_map/all_to_all | solution.py:288
  73.9 0.1 pad_add_fusion.where_ref
  74.0 0.0 copy-done.9
  74.0 0.0 copy-done.10
  74.0 4.2 %shard_map.74 = (f32[4,1024,512]{2,1,0:T(8,128)S(1)}, f32[8,128]{1,0:T(8,128)S(1)}) custom-call(s32[2]{0:T(128)S(1)} %pad_add_fusion.where_ref, bf16[256,2176]{1,0:T(8,128)(2,1)S(1)} %bitcast.11, f32[8,1024]{1,0:T(8,128)S(1)} %copy-done.10, f32[8,2048]{1,0:T(8,128)S(1)} %copy-done.9), custom_call_target="tpu_custom_call" | custom-call | flops 268435456 | bytes 8388608 | tf_op jit(solution)/shard_map/pallas_call | solution.py:149
  78.1 0.0 copy-start
  78.2 3.3 %copy-done = f32[4,1024,512]{2,1,0:T(8,128)} copy-done((f32[4,1024,512]{2,1,0:T(8,128)}, f32[4,1024,512]{2,1,0:T(8,128)S(1)}, u32[]{:S(2)}) %copy-start) | copy-done | bytes 8388632
  81.4 6.3 %all-to-all-done.1.parts_ref = f32[64,8,128]{2,1,0:T(8,128)S(1)} async-done(((f32[64,8,128]{2,1,0:T(8,128)}), f32[64,8,128]{2,1,0:T(8,128)S(1)}, u32[]{:S(2)}, u32[]{:S(2)}) %all-to-all-start.1) | async-done | bytes 262176 | tf_op jit(solution)/shard_map/all_to_all | solution.py:288
  87.7 0.0 all-gather.3.cloned.1.call-done.winv_ref
  87.7 0.0 copy-start.2
  87.7 1.2 copy-done.2
  89.0 0.6 shard_map.76
  89.6 8.1 %all_to_all.20.pieces_ref = f32[4,8,1024]{2,1,0:T(8,128)S(1)} all-to-all(f32[4,8,1024]{2,1,0:T(8,128)S(1)} %shard_map.76), channel_id=1, replica_groups=mesh['zh'=4,'y'=8,'core'=2,'x'=4,'zl'=2] {'x'}, dimensions={0} | all-to-all | bytes 262144 | tf_op jit(solution)/shard_map/all_to_all | solution.py:294
  97.7 0.0 copy-start.1
  97.7 3.4 %copy-done.1 = f32[4,1024,512]{2,1,0:T(8,128)S(1)} copy-done((f32[4,1024,512]{2,1,0:T(8,128)S(1)}, f32[4,1024,512]{2,1,0:T(8,128)}, u32[]{:S(2)}) %copy-start.1) | copy-done | bytes 8388632
  101.1 1.5 %shard_map.77 = bf16[64,2,8,128]{3,2,1,0:T(8,128)(2,1)S(1)} custom-call(f32[4,1024,512]{2,1,0:T(8,128)S(1)} %copy-done.1, f32[4,8,1024]{2,1,0:T(8,128)S(1)} %all_to_all.20.pieces_ref, f32[8,128]{1,0:T(8,128)S(1)} %get-tuple-element.9.after_ref.aux_ref), custom_call_target="tpu_custom_call" | custom-call | flops 4194304 | bytes 8388608 | tf_op jit(solution)/shard_map/pallas_call | solution.py:211
  102.6 24.7 %all_to_all.21 = bf16[128,8,128]{2,1,0:T(8,128)(2,1)S(1)} all-to-all(bf16[128,8,128]{2,1,0:T(8,128)(2,1)S(1)} %bitcast.14), channel_id=1, replica_groups=mesh['zh'=4,'y'=8,'core'=2,'x'=4,'zl'=2] {'zh','y','core','zl'}, dimensions={0} | all-to-all | bytes 524288 | tf_op jit(solution)/shard_map/all_to_all | solution.py:296
  127.3 1.2 copy-done.3
  128.6 2.8 %shard_map.78 = bf16[256,2048]{1,0:T(8,128)(2,1)} custom-call(s32[1]{0:T(128)} %bitcast.place_ref.refs_0_, bf16[64,2,8,128]{3,2,1,0:T(8,128)(2,1)S(1)} %bitcast.13, bf16[256,2176]{1,0:T(8,128)(2,1)S(1)} %bitcast.12, bf16[256,2048]{1,0:T(8,128)(2,1)S(1)} %copy-done.3), custom_call_target="tpu_custom_call" | custom-call | flops 536870912 | bytes 3145728 | tf_op jit(solution)/shard_map/pallas_call | solution.py:253
  (2 shorter events, 0.0 us)
Async XLA Ops:
  6.5 81.2 %all-gather.3.cloned.1.call-start = ((), (), s32[]{:S(2)}) async-start(), calls=%async_computation.4 | async-start | bytes 1179648 | tf_op jit(solution)/shard_map/all_gather | solution.py:285
  6.5 1.5 %collective-permute-start.1 = (f32[16,1024]{1,0:T(8,128)}, f32[16,1024]{1,0:T(8,128)S(1)}, u32[]{:S(2)}, u32[]{:S(2)}) collective-permute-start(f32[16,1024]{1,0:T(8,128)} %bitcast.18), channel_id=1, source_target_pairs={{0,0},{2,128},{4,256},{6,384},{128,2},{130,130},{132,258},{134,386... | collective-permute-start | bytes 196616 | tf_op jit(solution)/shard_map/ppermute | solution.py:281
  16.6 1.0 copy-start.5
  17.6 0.7 copy-start.7
  18.2 0.7 copy-start.8
  20.0 11.6 %copy-start.4 = (bf16[128,2048]{1,0:T(8,128)(2,1)S(1)}, bf16[128,2048]{1,0:T(8,128)(2,1)}, u32[]{:S(2)}) copy-start(bf16[128,2048]{1,0:T(8,128)(2,1)} %refs_0_.1) | copy-start | bytes 1572868
  20.0 27.8 %all-to-all-start = ((bf16[4,64,2176]{2,1,0:T(8,128)(2,1)}), bf16[4,64,2176]{2,1,0:T(8,128)(2,1)S(1)}, u32[]{:S(2)}, u32[]{:S(2)}) async-start(bf16[4,64,2176]{2,1,0:T(8,128)(2,1)} %shard_map.73), calls=%async_computation | async-start | bytes 2228224 | tf_op jit(solution)/shard_map/all_to_all | solution.py:278
  31.6 95.7 %all-gather.5.cloned.1.call-start = ((), (), s32[]{:S(2)}) async-start(), calls=%async_computation.5 | async-start | bytes 1310720 | tf_op jit(solution)/shard_map/all_gather | solution.py:292
  31.6 16.2 %collective-permute-start = (bf16[128,2048]{1,0:T(8,128)(2,1)S(1)}, bf16[128,2048]{1,0:T(8,128)(2,1)S(1)}, u32[]{:S(2)}, u32[]{:S(2)}) collective-permute-start(bf16[128,2048]{1,0:T(8,128)(2,1)S(1)} %copy-done.4), channel_id=1, source_target_pairs={{0,1},{1,0},{2,3},{3,2},{4,5},{5,4},{6,7},{7,6},{8,9},{9,8},{10,11... | collective-permute-start | bytes 1572872 | tf_op jit(solution)/shard_map/ppermute | solution.py:277
  47.8 1.4 %copy-start.6 = (bf16[2048,64]{0,1:T(8,128)(2,1)S(1)}, bf16[2048,64]{0,1:T(8,128)(2,1)}, u32[]{:S(2)}) copy-start(bf16[2048,64]{0,1:T(8,128)(2,1)} %param.8) | copy-start | bytes 786436
  47.8 26.1 %copy-start.9 = (f32[8,2048]{1,0:T(8,128)S(1)}, f32[8,2048]{1,0:T(8,128)}, u32[]{:S(2)}) copy-start(f32[8,2048]{1,0:T(8,128)} %new_ref.1) | copy-start | bytes 196612
  47.8 26.1 %copy-start.10 = (f32[8,1024]{1,0:T(8,128)S(1)}, f32[8,1024]{1,0:T(8,128)}, u32[]{:S(2)}) copy-start(f32[8,1024]{1,0:T(8,128)} %design_ref.1) | copy-start | bytes 98308
  49.3 8.6 %collective-permute-start.2 = (bf16[64,2048]{1,0:T(8,128)(2,1)S(1)}, bf16[64,2048]{1,0:T(8,128)(2,1)S(1)}, u32[]{:S(2)}, u32[]{:S(2)}) collective-permute-start(bf16[64,2048]{1,0:T(8,128)(2,1)S(1)} %bitcast.16), channel_id=1, source_target_pairs={{0,1},{1,0},{2,3},{3,2},{4,5},{5,4},{6,7},{7,6},{8,9},{9,8},{10,11... | collective-permute-start | bytes 786440 | tf_op jit(solution)/shard_map/ppermute | solution.py:292
  57.9 0.7 copy-start.11
  58.6 29.1 %all-to-all-start.1 = ((f32[64,8,128]{2,1,0:T(8,128)}), f32[64,8,128]{2,1,0:T(8,128)S(1)}, u32[]{:S(2)}, u32[]{:S(2)}) async-start(f32[64,8,128]{2,1,0:T(8,128)} %bitcast.6), calls=%async_computation.1 | async-start | bytes 524288 | tf_op jit(solution)/shard_map/all_to_all | solution.py:288
  78.1 3.3 %copy-start = (f32[4,1024,512]{2,1,0:T(8,128)}, f32[4,1024,512]{2,1,0:T(8,128)S(1)}, u32[]{:S(2)}) copy-start(f32[4,1024,512]{2,1,0:T(8,128)S(1)} %get-tuple-element.8.cross_ref) | copy-start | bytes 25165828
  87.7 1.2 copy-start.2
  97.7 3.4 %copy-start.1 = (f32[4,1024,512]{2,1,0:T(8,128)S(1)}, f32[4,1024,512]{2,1,0:T(8,128)}, u32[]{:S(2)}) copy-start(f32[4,1024,512]{2,1,0:T(8,128)} %copy-done) | copy-start | bytes 25165828
  127.3 1.2 copy-start.3
Sparse Core Ops, SparseCore 0:
  16.7 45.4 all-gather.2
  64.3 31.4 all-gather.4

commit v3 on v2

v3 whole, which is shorter than its diff:
```python
import math

import jax
import jax.numpy as jnp
from jax import lax
from jax.experimental import pallas as pl
from jax.experimental.pallas import tpu as pltpu
from jax.sharding import Mesh, PartitionSpec as P

GRID = ("zh", "y", "core")
COMP = ("x", "zl")
LOG2E = 1.4426950408889634
LN2 = 0.6931471805599453
F32 = jnp.float32
BF16 = jnp.bfloat16
HIGHEST = lax.Precision.HIGHEST
VMEM = pl.BlockSpec(memory_space=pltpu.VMEM)
SMEM = pl.BlockSpec(memory_space=pltpu.SMEM)
CELLS = 2048
WIDE = CELLS + 128


def params(mib):
    return pltpu.CompilerParams(vmem_limit_bytes=mib << 20)


def split3(value):
    first = value.astype(BF16)
    rest = value - first.astype(F32)
    second = rest.astype(BF16)
    third = (rest - second.astype(F32)).astype(BF16)
    return first, second, third


def pack_kernel(basis_ref, lscale_ref, variance_ref, out_ref):
    row = lax.broadcasted_iota(jnp.int32, (8, 64), 0)
    tail = jnp.where(row == 0, jnp.broadcast_to(variance_ref[...], (8, 64)), 0.0)
    value = jnp.concatenate([lscale_ref[...], tail], axis=0)
    pieces = jnp.concatenate([part.astype(F32) for part in split3(value)], axis=0)
    pieces = jnp.concatenate([pieces, jnp.zeros((80, 64), F32)], axis=0)
    side = jnp.concatenate([pieces, jnp.zeros((128, 64), F32)], axis=1).T[:64].astype(BF16)
    basis = basis_ref[...]
    for peer in range(4):
        out_ref[peer, :, :CELLS] = basis
        out_ref[peer, :, CELLS:] = side


def pack(basis, lscale, variance):
    return pl.pallas_call(
        pack_kernel,
        out_shape=jax.ShapeDtypeStruct((4, 64, WIDE), BF16),
        in_specs=[VMEM] * 3,
        out_specs=VMEM,
        compiler_params=params(16),
        cost_estimate=pl.CostEstimate(flops=0, bytes_accessed=5 << 18, transcendentals=0),
    )(basis, lscale, variance)


def project_kernel(scale, where_ref, own_ref, other_ref, basis_ref, pair_ref, out_ref, runs_ref, wide_ref):
    zl = where_ref[2]
    for half, fields_ref in ((zl, own_ref), (1 - zl, other_ref)):
        for y in range(4):
            for core in range(2):
                first = pl.multiple_of(128 * core + 64 * half + 16 * y, 16)
                from_row = 32 * y + 16 * core
                runs_ref[pl.ds(first, 16), :] = fields_ref[from_row : from_row + 16]
    part = lax.dot_general(
        basis_ref[:, :CELLS], runs_ref[...], (((1,), (1,)), ((), ())), preferred_element_type=F32
    )
    part = part * scale
    high = part.astype(BF16).astype(F32)
    lanes = pl.ds(pl.multiple_of(128 * where_ref[3], 128), 128)
    for half in range(2):
        for block in range(4):
            for core in range(2):
                first = 64 * block + 32 * core
                row = 16 * half + 4 * core + block
                piece = (slice(first, first + 32), slice(128 * half, 128 * half + 128))
                wide_ref[pl.ds(row, 32, stride=32), :] = high[piece]
                wide_ref[pl.ds(row + 8, 32, stride=32), :] = part[piece] - high[piece]
        mine = pair_ref[16 * half : 16 * half + 16, lanes]
        for chip in range(32):
            out_ref[2 * chip + half, 16:, :] = mine
    out_ref[:, :16, :] = wide_ref[...].astype(BF16).reshape(64, 16, 128)


def project(where, own, other, basis, pair, scale):
    def body(*refs):
        project_kernel(scale, *refs)

    return pl.pallas_call(
        body,
        out_shape=jax.ShapeDtypeStruct((64, 32, 128), BF16),
        in_specs=[SMEM] + [VMEM] * 4,
        out_specs=VMEM,
        scratch_shapes=[pltpu.VMEM((256, CELLS), BF16), pltpu.VMEM((1024, 128), F32)],
        compiler_params=params(16),
        cost_estimate=pl.CostEstimate(flops=1 << 28, bytes_accessed=1 << 21, transcendentals=0),
    )(where, own, other, basis, pair)


def weights_kernel(parts_ref, out_ref, winv_ref):
    for device in range(64):
        slot, y = 2 * (device // 16) + device % 2, device // 2 % 8
        winv_ref[16 * y : 16 * y + 16, 128 * slot : 128 * slot + 128] = parts_ref[device, 16:, :]
    both = jnp.sum(parts_ref[:, :16, :].astype(F32), axis=0)
    coef = both[:8] + both[8:]
    rows = jnp.concatenate(
        [p.astype(F32) for p in split3(coef)] + [jnp.zeros((8, 128), F32)], axis=0
    ).astype(BF16)
    full = jnp.dot(rows, winv_ref[...], preferred_element_type=F32)
    full = (full[16:24] + full[8:16]) + full[:8]
    for core in range(2):
        for block in range(4):
            for tile in range(8):
                piece = full[4 * core + block : 4 * core + block + 1, 128 * tile : 128 * tile + 128]
                for peer in range(4):
                    row = 8 * block + tile
                    out_ref[2 * peer + core, row : row + 1, :] = piece


def weights(parts):
    return pl.pallas_call(
        weights_kernel,
        out_shape=jax.ShapeDtypeStruct((8, 32, 128), F32),
        in_specs=[VMEM],
        out_specs=VMEM,
        scratch_shapes=[pltpu.VMEM((128, 1024), BF16)],
        compiler_params=params(16),
        cost_estimate=pl.CostEstimate(flops=1 << 23, bytes_accessed=1 << 20, transcendentals=0),
    )(parts)


def prepare_kernel(where_ref, side_ref, design_ref, new_ref, runs_ref, new_out_ref, aux_ref, wide_ref):
    wide_ref[...] = side_ref[...].astype(F32)
    runs = design_ref[...] - 0.5
    first, second, third = split3(jnp.concatenate([runs, runs * runs], axis=0))
    row = lax.broadcasted_iota(jnp.int32, (32, 1024), 0)
    ones = jnp.where(row < 3, 1.0, 0.0)
    parts = [first, first, first, second, second, third]
    table = jnp.concatenate([p.astype(F32) for p in parts] + [ones], axis=0)
    runs_ref[...] = table.T.astype(BF16)
    new = new_ref[:, pl.ds(pl.multiple_of(where_ref[0] * 512, 512), 512)] - 0.5
    aux_ref[...] = jnp.zeros((8, 128), F32)
    row = lax.broadcasted_iota(jnp.int32, (32, 512), 0)
    for block in range(4):
        mine = wide_ref[pl.ds(64 * block + where_ref[1], 1), :]
        column = jnp.broadcast_to(mine, (128, 128)).T
        value = (column[0:16] + column[16:32]) + column[32:48]
        aux_ref[block : block + 1, :] = value[8:9] * LN2
        lscale = value[:8]
        weight = (3.0 * LOG2E * LOG2E) / (lscale * lscale)
        weight = jnp.concatenate([weight] * 4, axis=1)
        scaled = weight * new
        first, second, third = split3(jnp.concatenate([-2.0 * scaled, weight], axis=0))
        square = jnp.broadcast_to(jnp.sum(scaled * new, axis=0, keepdims=True), (32, 512))
        lead, mid, low = [p.astype(F32) for p in split3(square)]
        tail = jnp.where(row == 0, lead, jnp.where(row == 1, mid, jnp.where(row == 2, low, 0.0)))
        new_out_ref[block] = jnp.concatenate(
            [first, second, third, first, second, first, tail.astype(BF16)], axis=0
        )


def prepare(where, basis, design, new_settings):
    return pl.pallas_call(
        prepare_kernel,
        grid=(1,),
        out_shape=(
            jax.ShapeDtypeStruct((1024, 128), BF16),
            jax.ShapeDtypeStruct((4, 128, 512), BF16),
            jax.ShapeDtypeStruct((8, 128), F32),
        ),
        in_specs=[
            SMEM,
            pl.BlockSpec((256, 128), lambda i: (0, CELLS // 128)),
            pl.BlockSpec((8, 1024), lambda i: (0, 0)),
            pl.BlockSpec((8, 2048), lambda i: (0, 0)),
        ],
        out_specs=(
            pl.BlockSpec((1024, 128), lambda i: (0, 0)),
            pl.BlockSpec((4, 128, 512), lambda i: (0, 0, 0)),
            pl.BlockSpec((8, 128), lambda i: (0, 0)),
        ),
        scratch_shapes=[pltpu.VMEM((256, 128), F32)],
        compiler_params=params(16),
        cost_estimate=pl.CostEstimate(flops=1 << 24, bytes_accessed=1 << 20, transcendentals=0),
    )(where, basis, design, new_settings)


def predict_kernel(runs_ref, new_ref, pieces_ref, aux_ref, out_ref, spread_ref, pred_ref):
    both = jnp.sum(pieces_ref[...], axis=0)
    parts = [p.astype(F32) for p in split3(both)]
    table = jnp.concatenate(parts + [jnp.zeros((32, 128), F32)], axis=0).T.astype(BF16)
    row = lax.broadcasted_iota(jnp.int32, (128, 512), 0)
    col = lax.broadcasted_iota(jnp.int32, (128, 512), 1)
    for tile in range(8):
        pick = ((row % 32 == 8 * (col // 128) + tile) & (row < 96)).astype(BF16)
        spread_ref[128 * tile : 128 * tile + 128, :] = jnp.dot(
            table, pick, preferred_element_type=F32
        )

    for block in range(4):
        acc = [jnp.zeros((8, 128), F32)] * 4
        for chunk in range(16):
            rows = slice(64 * chunk, 64 * chunk + 64)
            weight = spread_ref[rows, 128 * block : 128 * block + 128]
            sq = jnp.dot(runs_ref[rows], new_ref[block], preferred_element_type=F32)
            sq = jnp.maximum(sq, 1e-30)
            dist = sq * lax.rsqrt(sq)
            values = (LOG2E + dist) * jnp.exp2(-dist)
            for tile in range(4):
                prod = values[:, 128 * tile : 128 * tile + 128] * weight
                acc[tile] = acc[tile] + jnp.sum(prod.reshape(8, 8, 128), axis=0)
        for tile in range(4):
            where = (tile // 2) * 8 + 2 * block + tile % 2
            total = jnp.sum(acc[tile], axis=0, keepdims=True)
            pred_ref[where : where + 1, :] = total * aux_ref[block : block + 1, :]

    tile = pred_ref[...].astype(BF16).reshape(1, 2, 8, 128)
    out_ref[...] = jnp.broadcast_to(tile, (64, 2, 8, 128))


def predict(runs_feat, new_feat, pieces, aux):
    return pl.pallas_call(
        predict_kernel,
        out_shape=jax.ShapeDtypeStruct((64, 2, 8, 128), BF16),
        in_specs=[VMEM] * 4,
        out_specs=VMEM,
        scratch_shapes=[pltpu.VMEM((1024, 512), F32), pltpu.VMEM((16, 128), F32)],
        compiler_params=params(16),
        cost_estimate=pl.CostEstimate(
            flops=1 << 28, bytes_accessed=1 << 20, transcendentals=1 << 22
        ),
    )(runs_feat, new_feat, pieces, aux)


def rebuild_kernel(scale, where_ref, pred_ref, *refs):
    own_ref, other_ref, out_ref, wide_ref, lhs_ref = refs

    @pl.when(pl.program_id(0) == 0)
    def _():
        wide_ref[...] = pred_ref[...].astype(F32).reshape(1024, 128)
        zl = where_ref[2]
        for side, which in enumerate((zl, 1 - zl)):
            rows = []
            for block in range(4):
                first = 8 * which + 2 * block
                for core in range(2):
                    halves = [
                        wide_ref[pl.ds(16 * core + first + half, 32, stride=32), :]
                        for half in range(2)
                    ]
                    rows.append(jnp.concatenate(halves, axis=1))
            table = jnp.concatenate(rows, axis=0)
            lhs_ref[:, 256 * side : 256 * side + 256] = table.T.astype(BF16)

    total = jnp.dot(lhs_ref[:, :256], own_ref[...], preferred_element_type=F32)
    total = total + jnp.dot(lhs_ref[:, 256:], other_ref[...], preferred_element_type=F32)
    out_ref[...] = (total * scale).astype(BF16)


def rebuild(where, pred, own, other, scale):
    def body(*refs):
        rebuild_kernel(scale, *refs)

    width = 512
    return pl.pallas_call(
        body,
        grid=(CELLS // width,),
        out_shape=jax.ShapeDtypeStruct((256, CELLS), BF16),
        in_specs=[
            SMEM,
            pl.BlockSpec((64, 2, 8, 128), lambda i: (0, 0, 0, 0)),
            *[pl.BlockSpec((256, width), lambda i: (0, i))] * 2,
        ],
        out_specs=pl.BlockSpec((256, width), lambda i: (0, i)),
        scratch_shapes=[pltpu.VMEM((1024, 128), F32), pltpu.VMEM((256, 512), BF16)],
        compiler_params=params(16),
        cost_estimate=pl.CostEstimate(flops=1 << 29, bytes_accessed=3 << 20, transcendentals=0),
    )(where, pred, own, other)


def on_device(fields_runs, eof_basis, weights_inv, design, new_settings, lscale, variance):
    zh, core = lax.axis_index("zh"), lax.axis_index("core")
    column = 32 * core + 8 * zh + lax.axis_index("y")
    where = jnp.stack([lax.axis_index("x"), column, lax.axis_index("zl"), 2 * zh + core])
    swap = [(0, 1), (1, 0)]

    fields_other = lax.ppermute(fields_runs, "zl", swap)
    basis = lax.all_to_all(
        pack(eof_basis.T, lscale, variance.reshape(1, 64)), "x", 0, 0, tiled=True
    ).reshape(256, WIDE)
    pair = lax.all_gather(weights_inv.T.astype(BF16), "core", axis=0, tiled=True)
    pair = lax.ppermute(
        pair, ("zh", "x"), [(a * 4 + b, b * 4 + a) for a in range(4) for b in range(4)]
    )

    sent = project(where, fields_runs, fields_other, basis, pair, 1.0 / math.sqrt(131072))
    parts = lax.all_to_all(sent, GRID, 0, 0, tiled=True)

    runs_feat, new_feat, aux = prepare(where, basis, design, new_settings)
    basis_other = lax.ppermute(basis, "zl", swap)

    pieces = lax.all_to_all(weights(parts), ("x", "core"), 0, 0, tiled=True)
    pred = predict(runs_feat, new_feat, pieces, aux)
    pred = lax.all_to_all(pred.reshape(128, 8, 128), GRID + ("zl",), 0, 0, tiled=True)
    return rebuild(
        where, pred.reshape(64, 2, 8, 128), basis, basis_other, 1.0 / math.sqrt(512)
    )


def solution(mesh):
    fine = Mesh(mesh.devices.reshape(4, 8, 2, 4, 2), GRID + COMP)
    placed = (
        P(COMP, GRID),
        P(GRID, COMP),
        P(None, GRID),
        P(),
        P(),
        P(None, COMP),
        P(COMP),
    )
    return jax.shard_map(
        on_device, mesh=fine, in_specs=placed, out_specs=P(COMP, GRID), check_vma=False
    )
```

time: 139 us -> 109 us (0.78)
  blocking collectives: 41.4 us -> 5.01 us
  waiting for transfers between devices: 23.4 us -> 38 us
  starting transfers between devices: 36.2 us -> 50 us
  between operations: 13.5 us -> 0.1 us
  local copies, waits for them, and re-layouts: 12.1 us -> 2.31 us
    all_to_all x2 -> x0, blocking collectives: 32.9 us -> none  [the longest x1 24.7 us: on_device(): lax.all_to_all(pred.reshape(128, 8, 128), GRID + ('zl',), 0, 0, tiled=True)]
    all_to_all x2 -> x4, waiting for transfers between devices: 6.34 us -> 35.9 us  [the longest x1 16.6 us: on_device(): parts = lax.all_to_all(sent, GRID, 0, 0, tiled=True)]
    all_to_all x2 -> x4, starting transfers between devices: 26.9 us -> 43.5 us  [the longest x1 23.8 us: on_device(): parts = lax.all_to_all(sent, GRID, 0, 0, tiled=True)]
    unnamed x24 -> x14, local copies, waits for them, and re-layouts: 12.1 us -> 2.31 us
    ppermute x1, waiting for transfers between devices: 11.8 us -> 2.18 us  [on_device(): fields_other = lax.ppermute(fields_runs, 'zl', swap)]
    ppermute x2, waiting for transfers between devices: 5.2 us -> 0.01 us  [the longest x1 0.01 us: on_device(): lax.ppermute(pair, ('zh', 'x'), [(a * 4 + b, b * 4 + a) for a in range(4)...]
    all_gather x1, blocking collectives: 8.55 us -> 5.01 us  [on_device(): lax.all_gather(weights_inv.T.astype(BF16), 'core', axis=0, tiled=True)]
    ppermute x2, starting transfers between devices: 4.92 us -> 2.57 us  [the longest x1 1.92 us: on_device(): basis_other = lax.ppermute(basis, 'zl', swap)]
  transfers between devices with their start and end apart: 7 -> 7, of which waited for: 3 -> 4; matrix products, arithmetic and copies ran while one was open for 0% -> 0% of each run, Pallas kernels for 6% -> 5%
where the time goes in v3:
time: 109 us; the launch traced here: 108 us
  starting transfers between devices  50 us (46%)
  waiting for transfers between devices  38 us (35%)
  Pallas kernels  12.8 us (12%)
  blocking collectives  5.01 us (5%)
  local copies, waits for them, and re-layouts  2.31 us (2%)
    all_to_all x1, starting transfers between devices, on_device(): parts = lax.all_to_all(sent, GRID, 0, 0, tiled=True)  23.8 us
    all_to_all x1, waiting for transfers between devices, on_device(): parts = lax.all_to_all(sent, GRID, 0, 0, tiled=True)  16.6 us
    all_to_all x1, waiting for transfers between devices, on_device(): lax.all_to_all(pred.reshape(128, 8, 128), GRID + ('zl',), 0, 0, tiled=True)  14.8 us
    all_to_all x1, starting transfers between devices, on_device(): lax.all_to_all(pred.reshape(128, 8, 128), GRID + ('zl',), 0, 0, tiled=True)  8.45 us
    all_to_all x1, starting transfers between devices, on_device(): pieces = lax.all_to_all(weights(parts), ('x', 'core'), 0, 0, tiled=True)  6.25 us
    all_gather x1, blocking collectives, on_device(): lax.all_gather(weights_inv.T.astype(BF16), 'core', axis=0, tiled=True)  5.01 us
    all_to_all x1, starting transfers between devices, on_device(): lax.all_to_all(pack(eof_basis.T, lscale, variance.reshape(1, 64)), 'x', 0...  4.97 us
    all_to_all x1, waiting for transfers between devices, on_device(): pieces = lax.all_to_all(weights(parts), ('x', 'core'), 0, 0, tiled=True)  4.48 us
  transfers between devices with their start and end apart: 7, of which 4 were waited for; matrix products, arithmetic and copies ran while one was open for 0% of the time, Pallas kernels for 5%

profile of v3, /device:TPU:1, one launch (start us, length us, event | category | flops | bytes accessed | tf_op | source)
XLA Modules:
  0.0 108.4 jit_solution(2391240069363476248)
XLA Ops:
  0.0 0.0 copy-start.1
  0.0 0.9 copy-done.1
  1.0 0.0 copy-start.4
  1.0 0.7 copy-done.4
  1.6 0.0 copy-start.5
  1.6 0.7 copy-done.5
  2.3 1.1 %shard_map.73 = bf16[4,64,2176]{2,1,0:T(8,128)(2,1)} custom-call(bf16[64,2048]{1,0:T(8,128)(2,1)S(1)} %bitcast.16, f32[8,64]{1,0:T(8,128)S(1)} %copy-done.4, f32[1,64]{1,0:T(1,128)S(1)} %bitcast.17), custom_call_target="tpu_custom_call" | custom-call | bytes 1310720 | tf_op jit(solution)/shard_map/pallas_call | solution.py:49
  3.4 0.0 copy-start
  3.4 0.0 copy-start.6
  3.4 5.0 %all-to-all-start = ((bf16[4,64,2176]{2,1,0:T(8,128)(2,1)}), bf16[4,64,2176]{2,1,0:T(8,128)(2,1)S(1)}, u32[]{:S(2)}, u32[]{:S(2)}) async-start(bf16[4,64,2176]{2,1,0:T(8,128)(2,1)} %shard_map.73), calls=%async_computation | async-start | bytes 2228224 | tf_op jit(solution)/shard_map/all_to_all | solution.py:290
  8.4 0.0 copy-done
  8.4 4.0 %collective-permute-start = (bf16[128,2048]{1,0:T(8,128)(2,1)S(1)}, bf16[128,2048]{1,0:T(8,128)(2,1)S(1)}, u32[]{:S(2)}, u32[]{:S(2)}) collective-permute-start(bf16[128,2048]{1,0:T(8,128)(2,1)S(1)} %copy-done), channel_id=1, source_target_pairs={{0,1},{1,0},{2,3},{3,2},{4,5},{5,4},{6,7},{7,6},{8,9},{9,8},{10,11... | collective-permute-start | bytes 1572872 | tf_op jit(solution)/shard_map/ppermute | solution.py:289
  12.4 0.0 copy-done.6
  12.4 5.0 %all_gather.3 = bf16[32,1024]{1,0:T(8,128)(2,1)S(1)} all-gather(bf16[16,1024]{1,0:T(8,128)(2,1)S(1)} %convert_bitcast_fusion), channel_id=1, replica_groups=mesh['zh'=4,'y'=8,'core'=2,'x'=4,'zl'=2] {'core'}, dimensions={0}, use_global_device_ids=true | all-gather | bytes 98304 | tf_op jit(solution)/shard_map/all_gather | solution.py:293
  17.4 0.7 collective-permute-start.1
  18.1 0.1 pad_add_fusion.where_ref.refs_0_
  18.2 0.0 collective-permute-done.1.refs_4_
  18.2 2.2 %collective-permute-done.refs_2_ = bf16[128,2048]{1,0:T(8,128)(2,1)S(1)} collective-permute-done((bf16[128,2048]{1,0:T(8,128)(2,1)S(1)}, bf16[128,2048]{1,0:T(8,128)(2,1)S(1)}, u32[]{:S(2)}, u32[]{:S(2)}) %collective-permute-start) | collective-permute-done | bytes 524320 | tf_op jit(solution)/shard_map/ppermute | solution.py:289
  20.4 0.0 all-to-all-done
  20.4 2.3 %shard_map.75 = bf16[64,32,128]{2,1,0:T(8,128)(2,1)} custom-call(s32[4]{0:T(128)S(1)} %pad_add_fusion.where_ref.refs_0_, bf16[128,2048]{1,0:T(8,128)(2,1)S(1)} %copy-done, bf16[128,2048]{1,0:T(8,128)(2,1)S(1)} %collective-permute-done.refs_2_, bf16[256,2176]{1,0:T(8,128)(2,1)S(1)} %bitcast.11, bf16[32,1024]{1,0:T(8,128)(2,1)S(1)} %collective-permute-done.1.refs_4_), custom_call_target="tpu_custom_call" | custom-call | flops 268435456 | bytes 2097152 | tf_op jit(solution)/shard_map/pallas_call | solution.py:91
  22.7 0.0 copy-start.2
  22.7 0.0 copy-start.3
  22.7 23.8 %all-to-all-start.1 = ((bf16[64,32,128]{2,1,0:T(8,128)(2,1)}), bf16[64,32,128]{2,1,0:T(8,128)(2,1)S(1)}, u32[]{:S(2)}, u32[]{:S(2)}) async-start(bf16[64,32,128]{2,1,0:T(8,128)(2,1)} %shard_map.75), calls=%async_computation.1 | async-start | bytes 1048576 | tf_op jit(solution)/shard_map/all_to_all | solution.py:299
  46.5 1.9 %collective-permute-start.2 = (bf16[256,2176]{1,0:T(8,128)(2,1)S(1)}, bf16[256,2176]{1,0:T(8,128)(2,1)S(1)}, u32[]{:S(2)}, u32[]{:S(2)}) collective-permute-start(bf16[256,2176]{1,0:T(8,128)(2,1)S(1)} %bitcast.12), channel_id=1, source_target_pairs={{0,1},{1,0},{2,3},{3,2},{4,5},{5,4},{6,7},{7,6},{8,9},{9,8},{10,11... | collective-permute-start | bytes 3342344 | tf_op jit(solution)/shard_map/ppermute | solution.py:302
  48.4 16.6 %all-to-all-done.1.parts_ref = bf16[64,32,128]{2,1,0:T(8,128)(2,1)S(1)} async-done(((bf16[64,32,128]{2,1,0:T(8,128)(2,1)}), bf16[64,32,128]{2,1,0:T(8,128)(2,1)S(1)}, u32[]{:S(2)}, u32[]{:S(2)}) %all-to-all-start.1) | async-done | bytes 524320 | tf_op jit(solution)/shard_map/all_to_all | solution.py:299
  65.0 0.9 shard_map.76
  66.0 6.2 %all-to-all-start.2 = ((f32[8,32,128]{2,1,0:T(8,128)}), f32[8,32,128]{2,1,0:T(8,128)S(1)}, u32[]{:S(2)}, u32[]{:S(2)}) async-start(f32[8,32,128]{2,1,0:T(8,128)} %shard_map.76), calls=%async_computation.2 | async-start | bytes 262144 | tf_op jit(solution)/shard_map/all_to_all | solution.py:304
  72.2 0.0 copy-done.2
  72.2 0.0 copy-done.3
  72.2 0.8 shard_map.74
  73.0 4.5 %all-to-all-done.2.pieces_ref = f32[8,32,128]{2,1,0:T(8,128)S(1)} async-done(((f32[8,32,128]{2,1,0:T(8,128)}), f32[8,32,128]{2,1,0:T(8,128)S(1)}, u32[]{:S(2)}, u32[]{:S(2)}) %all-to-all-start.2) | async-done | bytes 131104 | tf_op jit(solution)/shard_map/all_to_all | solution.py:304
  77.5 4.2 %shard_map.77 = bf16[64,2,8,128]{3,2,1,0:T(8,128)(2,1)} custom-call(bf16[1024,128]{1,0:T(8,128)(2,1)S(1)} %get-tuple-element.8.runs_ref, bf16[4,128,512]{2,1,0:T(8,128)(2,1)S(1)} %get-tuple-element.9.new_ref, f32[8,32,128]{2,1,0:T(8,128)S(1)} %all-to-all-done.2.pieces_ref, f32[8,128]{1,0:T(8,128)S(1)} %get-tuple-element.10.aux_ref), custom_call_target="tpu_custom_call" | custom-call | flops 268435456 | bytes 1048576 | tf_op jit(solution)/shard_map/pallas_call | solution.py:224
  81.7 8.4 %all-to-all-start.3 = ((bf16[128,8,128]{2,1,0:T(8,128)(2,1)}), bf16[128,8,128]{2,1,0:T(8,128)(2,1)S(1)}, u32[]{:S(2)}, u32[]{:S(2)}) async-start(bf16[128,8,128]{2,1,0:T(8,128)(2,1)} %bitcast.8), calls=%async_computation.3 | async-start | bytes 524288 | tf_op jit(solution)/shard_map/all_to_all | solution.py:306
  90.1 0.0 collective-permute-done.2.refs_3_
  90.2 14.8 %all-to-all-done.3 = bf16[128,8,128]{2,1,0:T(8,128)(2,1)S(1)} async-done(((bf16[128,8,128]{2,1,0:T(8,128)(2,1)}), bf16[128,8,128]{2,1,0:T(8,128)(2,1)S(1)}, u32[]{:S(2)}, u32[]{:S(2)}) %all-to-all-start.3) | async-done | bytes 262176 | tf_op jit(solution)/shard_map/all_to_all | solution.py:306
  104.9 3.5 %shard_map.78 = bf16[256,2048]{1,0:T(8,128)(2,1)} custom-call(s32[4]{0:T(128)S(1)} %pad_add_fusion.where_ref.refs_0_, bf16[64,2,8,128]{3,2,1,0:T(8,128)(2,1)S(1)} %bitcast.15, bf16[256,2176]{1,0:T(8,128)(2,1)S(1)} %bitcast.14, bf16[256,2176]{1,0:T(8,128)(2,1)S(1)} %collective-permute-done.2.refs_3_), custom_call_target="tpu_custom_call" | custom-call | flops 536870912 | bytes 3145728 | tf_op jit(solution)/shard_map/pallas_call | solution.py:267
  (1 shorter events, 0.0 us)
Async XLA Ops:
  0.0 0.9 copy-start.1
  1.0 0.7 copy-start.4
  1.6 0.7 copy-start.5
  3.4 5.0 %copy-start = (bf16[128,2048]{1,0:T(8,128)(2,1)S(1)}, bf16[128,2048]{1,0:T(8,128)(2,1)}, u32[]{:S(2)}) copy-start(bf16[128,2048]{1,0:T(8,128)(2,1)} %refs_1_.1) | copy-start | bytes 1572868
  3.4 9.0 %copy-start.6 = (f32[1024,16]{0,1:T(8,128)S(1)}, f32[1024,16]{0,1:T(8,128)}, u32[]{:S(2)}) copy-start(f32[1024,16]{0,1:T(8,128)} %param.9) | copy-start | bytes 196612
  3.4 16.9 %all-to-all-start = ((bf16[4,64,2176]{2,1,0:T(8,128)(2,1)}), bf16[4,64,2176]{2,1,0:T(8,128)(2,1)S(1)}, u32[]{:S(2)}, u32[]{:S(2)}) async-start(bf16[4,64,2176]{2,1,0:T(8,128)(2,1)} %shard_map.73), calls=%async_computation | async-start | bytes 2228224 | tf_op jit(solution)/shard_map/all_to_all | solution.py:290
  8.4 12.0 %collective-permute-start = (bf16[128,2048]{1,0:T(8,128)(2,1)S(1)}, bf16[128,2048]{1,0:T(8,128)(2,1)S(1)}, u32[]{:S(2)}, u32[]{:S(2)}) collective-permute-start(bf16[128,2048]{1,0:T(8,128)(2,1)S(1)} %copy-done), channel_id=1, source_target_pairs={{0,1},{1,0},{2,3},{3,2},{4,5},{5,4},{6,7},{7,6},{8,9},{9,8},{10,11... | collective-permute-start | bytes 1572872 | tf_op jit(solution)/shard_map/ppermute | solution.py:289
  17.4 0.8 collective-permute-start.1
  22.7 49.6 %copy-start.2 = (f32[8,2048]{1,0:T(8,128)S(1)}, f32[8,2048]{1,0:T(8,128)}, u32[]{:S(2)}) copy-start(f32[8,2048]{1,0:T(8,128)} %new_ref.1) | copy-start | bytes 196612
  22.7 49.6 %copy-start.3 = (f32[8,1024]{1,0:T(8,128)S(1)}, f32[8,1024]{1,0:T(8,128)}, u32[]{:S(2)}) copy-start(f32[8,1024]{1,0:T(8,128)} %design_ref.1) | copy-start | bytes 98308
  22.7 42.4 %all-to-all-start.1 = ((bf16[64,32,128]{2,1,0:T(8,128)(2,1)}), bf16[64,32,128]{2,1,0:T(8,128)(2,1)S(1)}, u32[]{:S(2)}, u32[]{:S(2)}) async-start(bf16[64,32,128]{2,1,0:T(8,128)(2,1)} %shard_map.75), calls=%async_computation.1 | async-start | bytes 1048576 | tf_op jit(solution)/shard_map/all_to_all | solution.py:299
  46.5 43.7 %collective-permute-start.2 = (bf16[256,2176]{1,0:T(8,128)(2,1)S(1)}, bf16[256,2176]{1,0:T(8,128)(2,1)S(1)}, u32[]{:S(2)}, u32[]{:S(2)}) collective-permute-start(bf16[256,2176]{1,0:T(8,128)(2,1)S(1)} %bitcast.12), channel_id=1, source_target_pairs={{0,1},{1,0},{2,3},{3,2},{4,5},{5,4},{6,7},{7,6},{8,9},{9,8},{10,11... | collective-permute-start | bytes 3342344 | tf_op jit(solution)/shard_map/ppermute | solution.py:302
  66.0 11.5 %all-to-all-start.2 = ((f32[8,32,128]{2,1,0:T(8,128)}), f32[8,32,128]{2,1,0:T(8,128)S(1)}, u32[]{:S(2)}, u32[]{:S(2)}) async-start(f32[8,32,128]{2,1,0:T(8,128)} %shard_map.76), calls=%async_computation.2 | async-start | bytes 262144 | tf_op jit(solution)/shard_map/all_to_all | solution.py:304
  81.7 23.2 %all-to-all-start.3 = ((bf16[128,8,128]{2,1,0:T(8,128)(2,1)}), bf16[128,8,128]{2,1,0:T(8,128)(2,1)S(1)}, u32[]{:S(2)}, u32[]{:S(2)}) async-start(bf16[128,8,128]{2,1,0:T(8,128)(2,1)} %bitcast.8), calls=%async_computation.3 | async-start | bytes 524288 | tf_op jit(solution)/shard_map/all_to_all | solution.py:306

commit v4 on v3

--- a/solution.py
+++ b/solution.py
@@ -51,58 +51,82 @@
         out_shape=jax.ShapeDtypeStruct((4, 64, WIDE), BF16),
         in_specs=[VMEM] * 3,
         out_specs=VMEM,
-        compiler_params=params(16),
+        compiler_params=params(60),
         cost_estimate=pl.CostEstimate(flops=0, bytes_accessed=5 << 18, transcendentals=0),
     )(basis, lscale, variance)
 
 
-def project_kernel(scale, where_ref, own_ref, other_ref, basis_ref, pair_ref, out_ref, runs_ref, wide_ref):
+def project_kernel(scale, where_ref, own_ref, other_ref, basis_ref, mine_ref, theirs_ref, runs_ref):
     zl = where_ref[2]
+    core = where_ref[4]
     for half, fields_ref in ((zl, own_ref), (1 - zl, other_ref)):
         for y in range(4):
-            for core in range(2):
-                first = pl.multiple_of(128 * core + 64 * half + 16 * y, 16)
-                from_row = 32 * y + 16 * core
-                runs_ref[pl.ds(first, 16), :] = fields_ref[from_row : from_row + 16]
+            for side in range(2):
+                first = 128 * lax.rem(side + core, 2) + 64 * half + 16 * y
+                from_row = 32 * y + 16 * side
+                runs_ref[pl.ds(pl.multiple_of(first, 16), 16), :] = fields_ref[
+                    from_row : from_row + 16
+                ]
     part = lax.dot_general(
         basis_ref[:, :CELLS], runs_ref[...], (((1,), (1,)), ((), ())), preferred_element_type=F32
     )
-    part = part * scale
-    high = part.astype(BF16).astype(F32)
-    lanes = pl.ds(pl.multiple_of(128 * where_ref[3], 128), 128)
-    for half in range(2):
-        for block in range(4):
-            for core in range(2):
-                first = 64 * block + 32 * core
-                row = 16 * half + 4 * core + block
-                piece = (slice(first, first + 32), slice(128 * half, 128 * half + 128))
-                wide_ref[pl.ds(row, 32, stride=32), :] = high[piece]
-                wide_ref[pl.ds(row + 8, 32, stride=32), :] = part[piece] - high[piece]
-        mine = pair_ref[16 * half : 16 * half + 16, lanes]
-        for chip in range(32):
-            out_ref[2 * chip + half, 16:, :] = mine
-    out_ref[:, :16, :] = wide_ref[...].astype(BF16).reshape(64, 16, 128)
-
-
-def project(where, own, other, basis, pair, scale):
+    mine_ref[...] = part[:, :128] * scale
+    theirs_ref[...] = part[:, 128:] * scale
+
+
+def project(where, own, other, basis, scale):
     def body(*refs):
         project_kernel(scale, *refs)
 
+    half = jax.ShapeDtypeStruct((256, 128), F32)
     return pl.pallas_call(
         body,
-        out_shape=jax.ShapeDtypeStruct((64, 32, 128), BF16),
-        in_specs=[SMEM] + [VMEM] * 4,
+        out_shape=(half, half),
+        in_specs=[SMEM] + [VMEM] * 3,
+        out_specs=(VMEM, VMEM),
+        scratch_shapes=[pltpu.VMEM((256, CELLS), BF16)],
+        compiler_params=params(16),
+        cost_estimate=pl.CostEstimate(flops=1 << 28, bytes_accessed=1 << 21, transcendentals=0),
+    )(where, own, other, basis)
+
+
+def slots_kernel(where_ref, mine_ref, theirs_ref, block_ref, out_ref, wide_ref):
+    part = mine_ref[...] + theirs_ref[1 - where_ref[4]]
+    high = part.astype(BF16).astype(F32)
+    low = part - high
+    for block in range(4):
+        for core in range(2):
+            first = 64 * block + 32 * core
+            row = 4 * core + block
+            wide_ref[pl.ds(row, 32, stride=16), :] = high[first : first + 32]
+            wide_ref[pl.ds(row + 8, 32, stride=16), :] = low[first : first + 32]
+    out_ref[:, :16, :] = wide_ref[...].astype(BF16).reshape(32, 16, 128)
+    for side in range(2):
+        lanes = pl.ds(pl.multiple_of(256 * where_ref[3] + 128 * side, 128), 128)
+        piece = block_ref[:, lanes]
+        for chip in range(32):
+            out_ref[chip, 16 + 16 * side : 32 + 16 * side, :] = piece
+
+
+def slots(where, mine, theirs, block):
+    return pl.pallas_call(
+        slots_kernel,
+        out_shape=jax.ShapeDtypeStruct((32, 48, 128), BF16),
+        in_specs=[SMEM] + [VMEM] * 3,
         out_specs=VMEM,
-        scratch_shapes=[pltpu.VMEM((256, CELLS), BF16), pltpu.VMEM((1024, 128), F32)],
-        compiler_params=params(16),
-        cost_estimate=pl.CostEstimate(flops=1 << 28, bytes_accessed=1 << 21, transcendentals=0),
-    )(where, own, other, basis, pair)
+        scratch_shapes=[pltpu.VMEM((512, 128), F32)],
+        compiler_params=params(16),
+        cost_estimate=pl.CostEstimate(flops=1 << 20, bytes_accessed=1 << 20, transcendentals=0),
+    )(where, mine, theirs, block)
 
 
 def weights_kernel(parts_ref, out_ref, winv_ref):
-    for device in range(64):
-        slot, y = 2 * (device // 16) + device % 2, device // 2 % 8
-        winv_ref[16 * y : 16 * y + 16, 128 * slot : 128 * slot + 128] = parts_ref[device, 16:, :]
+    for chip in range(32):
+        zh, y = chip // 8, chip % 8
+        for side in range(2):
+            winv_ref[16 * y : 16 * y + 16, 256 * zh + 128 * side : 256 * zh + 128 * side + 128] = (
+                parts_ref[chip, 16 + 16 * side : 32 + 16 * side, :]
+            )
     both = jnp.sum(parts_ref[:, :16, :].astype(F32), axis=0)
     coef = both[:8] + both[8:]
     rows = jnp.concatenate(
@@ -217,13 +241,13 @@
             pred_ref[where : where + 1, :] = total * aux_ref[block : block + 1, :]
 
     tile = pred_ref[...].astype(BF16).reshape(1, 2, 8, 128)
-    out_ref[...] = jnp.broadcast_to(tile, (64, 2, 8, 128))
+    out_ref[...] = jnp.broadcast_to(tile, (32, 2, 8, 128))
 
 
 def predict(runs_feat, new_feat, pieces, aux):
     return pl.pallas_call(
         predict_kernel,
-        out_shape=jax.ShapeDtypeStruct((64, 2, 8, 128), BF16),
+        out_shape=jax.ShapeDtypeStruct((32, 2, 8, 128), BF16),
         in_specs=[VMEM] * 4,
         out_specs=VMEM,
         scratch_shapes=[pltpu.VMEM((1024, 512), F32), pltpu.VMEM((16, 128), F32)],
@@ -234,47 +258,52 @@
     )(runs_feat, new_feat, pieces, aux)
 
 
-def rebuild_kernel(scale, where_ref, pred_ref, *refs):
-    own_ref, other_ref, out_ref, wide_ref, lhs_ref = refs
-
-    @pl.when(pl.program_id(0) == 0)
-    def _():
-        wide_ref[...] = pred_ref[...].astype(F32).reshape(1024, 128)
-        zl = where_ref[2]
-        for side, which in enumerate((zl, 1 - zl)):
-            rows = []
-            for block in range(4):
-                first = 8 * which + 2 * block
-                for core in range(2):
-                    halves = [
-                        wide_ref[pl.ds(16 * core + first + half, 32, stride=32), :]
-                        for half in range(2)
-                    ]
-                    rows.append(jnp.concatenate(halves, axis=1))
-            table = jnp.concatenate(rows, axis=0)
-            lhs_ref[:, 256 * side : 256 * side + 256] = table.T.astype(BF16)
-
-    total = jnp.dot(lhs_ref[:, :256], own_ref[...], preferred_element_type=F32)
-    total = total + jnp.dot(lhs_ref[:, 256:], other_ref[...], preferred_element_type=F32)
-    out_ref[...] = (total * scale).astype(BF16)
+def rebuild_kernel(
+    scale, where_ref, pred_ref, own_ref, other_ref, out_ref, wide_ref, lhs_ref, done_ref, sems
+):
+    wide_ref[...] = pred_ref[...].astype(F32).reshape(1024, 128)
+    zl = where_ref[2]
+    for side, which in enumerate((zl, 1 - zl)):
+        rows = []
+        for block in range(4):
+            first = 8 * which + 2 * block
+            for core in range(2):
+                halves = [
+                    wide_ref[pl.ds(512 * core + first + half, 32, stride=16), :]
+                    for half in range(2)
+                ]
+                rows.append(jnp.concatenate(halves, axis=1))
+        table = jnp.concatenate(rows, axis=0)
+        lhs_ref[:, 256 * side : 256 * side + 256] = table.T.astype(BF16)
+
+    copies = []
+    for chunk in range(4):
+        cells = slice(512 * chunk, 512 * chunk + 512)
+        total = jnp.dot(lhs_ref[:, :256], own_ref[:, cells], preferred_element_type=F32)
+        total = total + jnp.dot(lhs_ref[:, 256:], other_ref[:, cells], preferred_element_type=F32)
+        done_ref[:, cells] = (total * scale).astype(BF16)
+        copy = pltpu.make_async_copy(done_ref.at[:, cells], out_ref.at[:, cells], sems.at[chunk])
+        copy.start()
+        copies.append(copy)
+    for copy in copies:
+        copy.wait()
 
 
 def rebuild(where, pred, own, other, scale):
     def body(*refs):
         rebuild_kernel(scale, *refs)
 
-    width = 512
     return pl.pallas_call(
         body,
-        grid=(CELLS // width,),
         out_shape=jax.ShapeDtypeStruct((256, CELLS), BF16),
-        in_specs=[
-            SMEM,
-            pl.BlockSpec((64, 2, 8, 128), lambda i: (0, 0, 0, 0)),
-            *[pl.BlockSpec((256, width), lambda i: (0, i))] * 2,
+        in_specs=[SMEM] + [VMEM] * 3,
+        out_specs=pl.BlockSpec(memory_space=pl.ANY),
+        scratch_shapes=[
+            pltpu.VMEM((1024, 128), F32),
+            pltpu.VMEM((256, 512), BF16),
+            pltpu.VMEM((256, CELLS), BF16),
+            pltpu.SemaphoreType.DMA((4,)),
         ],
-        out_specs=pl.BlockSpec((256, width), lambda i: (0, i)),
-        scratch_shapes=[pltpu.VMEM((1024, 128), F32), pltpu.VMEM((256, 512), BF16)],
         compiler_params=params(16),
         cost_estimate=pl.CostEstimate(flops=1 << 29, bytes_accessed=3 << 20, transcendentals=0),
     )(where, pred, own, other)
@@ -283,27 +312,30 @@
 def on_device(fields_runs, eof_basis, weights_inv, design, new_settings, lscale, variance):
     zh, core = lax.axis_index("zh"), lax.axis_index("core")
     column = 32 * core + 8 * zh + lax.axis_index("y")
-    where = jnp.stack([lax.axis_index("x"), column, lax.axis_index("zl"), 2 * zh + core])
+    where = jnp.stack([lax.axis_index("x"), column, lax.axis_index("zl"), zh, core])
     swap = [(0, 1), (1, 0)]
 
     fields_other = lax.ppermute(fields_runs, "zl", swap)
     basis = lax.all_to_all(
         pack(eof_basis.T, lscale, variance.reshape(1, 64)), "x", 0, 0, tiled=True
     ).reshape(256, WIDE)
-    pair = lax.all_gather(weights_inv.T.astype(BF16), "core", axis=0, tiled=True)
-    pair = lax.ppermute(
-        pair, ("zh", "x"), [(a * 4 + b, b * 4 + a) for a in range(4) for b in range(4)]
-    )
-
-    sent = project(where, fields_runs, fields_other, basis, pair, 1.0 / math.sqrt(131072))
-    parts = lax.all_to_all(sent, GRID, 0, 0, tiled=True)
+    block = lax.ppermute(
+        weights_inv.T.astype(BF16),
+        ("zh", "x"),
+        [(a * 4 + b, b * 4 + a) for a in range(4) for b in range(4)],
+    )
+
+    mine, theirs = project(where, fields_runs, fields_other, basis, 1.0 / math.sqrt(131072))
+    theirs = lax.all_gather(theirs, "core", axis=0)
+    parts = lax.all_to_all(slots(where, mine, theirs, block), ("zh", "y"), 0, 0, tiled=True)
 
     runs_feat, new_feat, aux = prepare(where, basis, design, new_settings)
     basis_other = lax.ppermute(basis, "zl", swap)
 
     pieces = lax.all_to_all(weights(parts), ("x", "core"), 0, 0, tiled=True)
     pred = predict(runs_feat, new_feat, pieces, aux)
-    pred = lax.all_to_all(pred.reshape(128, 8, 128), GRID + ("zl",), 0, 0, tiled=True)
+    pred = lax.all_to_all(pred.reshape(64, 8, 128), ("zh", "y", "zl"), 0, 0, tiled=True)
+    pred = lax.all_gather(pred, "core", axis=0, tiled=True)
     return rebuild(
         where, pred.reshape(64, 2, 8, 128), basis, basis_other, 1.0 / math.sqrt(512)
     )

time: 109 us -> 99.2 us (0.910)
  blocking collectives: 5.01 us -> 27.9 us
  starting transfers between devices: 50 us -> 34.9 us
  waiting for transfers between devices: 38 us -> 23.9 us
  local copies, waits for them, and re-layouts: 2.31 us -> 0.1 us
    all_to_all x2 -> x1, waiting for transfers between devices: 31.4 us -> 12.3 us  [on_device(): lax.all_to_all(slots(where, mine, theirs, block), ('zh', 'y'), 0, 0, tile...]
    all_to_all x0 -> x1, blocking collectives: none -> 16.8 us  [on_device(): lax.all_to_all(pred.reshape(64, 8, 128), ('zh', 'y', 'zl'), 0, 0, tiled=T...]
    all_to_all x2 -> x1, starting transfers between devices: 32.3 us -> 16.2 us  [on_device(): lax.all_to_all(slots(where, mine, theirs, block), ('zh', 'y'), 0, 0, tile...]
    all_gather x1 -> x2, blocking collectives: 5.01 us -> 11.1 us  [the longest x1 7.23 us: on_device(): theirs = lax.all_gather(theirs, 'core', axis=0)]
    ppermute x1, waiting for transfers between devices: 2.18 us -> 7.18 us  [on_device(): fields_other = lax.ppermute(fields_runs, 'zl', swap)]
    unnamed x14 -> x8, local copies, waits for them, and re-layouts: 2.31 us -> 0.01 us
    pallas_call x3 -> x4, Pallas kernels: 9.96 us -> 8.07 us  [the longest x1 3.42 us: predict(): pl.pallas_call(predict_kernel, out_shape=jax.ShapeDtypeStruct((32, 2, 8,...]
  transfers between devices with their start and end apart: 7 -> 6, of which waited for: 4 -> 3; matrix products, arithmetic and copies ran while one was open for 0% -> 0% of each run, Pallas kernels for 5% -> 6%
where the time goes in v4:
time: 99.2 us; the launch traced here: 98.8 us
  starting transfers between devices  34.9 us (35%)
  blocking collectives  27.9 us (28%)
  waiting for transfers between devices  23.9 us (24%)
  Pallas kernels  11.8 us (12%)
    all_to_all x1, blocking collectives, on_device(): lax.all_to_all(pred.reshape(64, 8, 128), ('zh', 'y', 'zl'), 0, 0, tiled=T...  16.8 us
    all_to_all x1, starting transfers between devices, on_device(): lax.all_to_all(slots(where, mine, theirs, block), ('zh', 'y'), 0, 0, tile...  16.2 us
    all_to_all x1, waiting for transfers between devices, on_device(): lax.all_to_all(slots(where, mine, theirs, block), ('zh', 'y'), 0, 0, tile...  12.3 us
    all_gather x1, blocking collectives, on_device(): theirs = lax.all_gather(theirs, 'core', axis=0)  7.23 us
    ppermute x1, waiting for transfers between devices, on_device(): fields_other = lax.ppermute(fields_runs, 'zl', swap)  7.18 us
    all_to_all x1, starting transfers between devices, on_device(): pieces = lax.all_to_all(weights(parts), ('x', 'core'), 0, 0, tiled=True)  6.61 us
    all_to_all x1, starting transfers between devices, on_device(): lax.all_to_all(pack(eof_basis.T, lscale, variance.reshape(1, 64)), 'x', 0...  4.97 us
    all_to_all x1, waiting for transfers between devices, on_device(): pieces = lax.all_to_all(weights(parts), ('x', 'core'), 0, 0, tiled=True)  4.48 us
  transfers between devices with their start and end apart: 6, of which 3 were waited for; matrix products, arithmetic and copies ran while one was open for 0% of the time, Pallas kernels for 6%

profile of v4, /device:TPU:1, one launch (start us, length us, event | category | flops | bytes accessed | tf_op | source)
XLA Modules:
  0.0 98.8 jit_solution(14724845539276216326)
XLA Ops:
  0.0 2.1 %shard_map.73 = bf16[4,64,2176]{2,1,0:T(8,128)(2,1)} custom-call(bf16[64,2048]{1,0:T(8,128)(2,1)} %bitcast.20, f32[8,64]{1,0:T(8,128)} %lscale_ref.1, f32[1,64]{1,0:T(1,128)} %bitcast.21), custom_call_target="tpu_custom_call" | custom-call | bytes 1310720 | tf_op jit(solution)/shard_map/pallas_call | solution.py:49
  2.1 0.0 copy-start
  2.1 0.0 copy-start.3
  2.1 5.0 %all-to-all-start = ((bf16[4,64,2176]{2,1,0:T(8,128)(2,1)}), bf16[4,64,2176]{2,1,0:T(8,128)(2,1)S(1)}, u32[]{:S(2)}, u32[]{:S(2)}) async-start(bf16[4,64,2176]{2,1,0:T(8,128)(2,1)} %shard_map.73), calls=%async_computation | async-start | bytes 2228224 | tf_op jit(solution)/shard_map/all_to_all | solution.py:319
  7.0 0.0 copy-done
  7.0 4.0 %collective-permute-start = (bf16[128,2048]{1,0:T(8,128)(2,1)S(1)}, bf16[128,2048]{1,0:T(8,128)(2,1)S(1)}, u32[]{:S(2)}, u32[]{:S(2)}) collective-permute-start(bf16[128,2048]{1,0:T(8,128)(2,1)S(1)} %copy-done), channel_id=1, source_target_pairs={{0,1},{1,0},{2,3},{3,2},{4,5},{5,4},{6,7},{7,6},{8,9},{9,8},{10,11... | collective-permute-start | bytes 1572872 | tf_op jit(solution)/shard_map/ppermute | solution.py:318
  11.0 0.0 copy-done.3
  11.1 0.7 collective-permute-start.1
  11.7 0.1 stack.23.where_ref.refs_0_
  11.8 7.2 %collective-permute-done.refs_2_ = bf16[128,2048]{1,0:T(8,128)(2,1)S(1)} collective-permute-done((bf16[128,2048]{1,0:T(8,128)(2,1)S(1)}, bf16[128,2048]{1,0:T(8,128)(2,1)S(1)}, u32[]{:S(2)}, u32[]{:S(2)}) %collective-permute-start) | collective-permute-done | bytes 524320 | tf_op jit(solution)/shard_map/ppermute | solution.py:318
  19.0 0.0 all-to-all-done
  19.0 1.1 %shard_map.75 = (f32[256,128]{1,0:T(8,128)S(1)}, f32[256,128]{1,0:T(8,128)S(1)}) custom-call(s32[5]{0:T(128)S(1)} %stack.23.where_ref.refs_0_, bf16[128,2048]{1,0:T(8,128)(2,1)S(1)} %copy-done, bf16[128,2048]{1,0:T(8,128)(2,1)S(1)} %collective-permute-done.refs_2_, bf16[256,2176]{1,0:T(8,128)(2,1)S(1)} %bitcast.13), custom_call_target="tpu_custom_call" | custom-call | flops 268435456 | bytes 2097152 | tf_op jit(solution)/shard_map/pallas_call | solution.py:82
  20.1 7.2 %all-gather = f32[512,128]{1,0:T(8,128)S(1)} all-gather(f32[256,128]{1,0:T(8,128)S(1)} %get-tuple-element.13), channel_id=2, replica_groups=mesh['zh'=4,'y'=8,'core'=2,'x'=4,'zl'=2] {'core'}, dimensions={0}, use_global_device_ids=true | all-gather | bytes 393216 | tf_op jit(solution)/shard_map/all_gather | solution.py:329
  27.3 0.0 collective-permute-done.1.block_ref
  27.3 0.0 copy-start.1
  27.3 0.0 copy-start.2
  27.3 1.4 %shard_map.76 = bf16[32,48,128]{2,1,0:T(8,128)(2,1)} custom-call(s32[5]{0:T(128)S(1)} %stack.23.where_ref.refs_0_, f32[256,128]{1,0:T(8,128)S(1)} %get-tuple-element.12.mine_ref, f32[2,256,128]{2,1,0:T(8,128)S(1)} %bitcast.17, bf16[16,1024]{1,0:T(8,128)(2,1)S(1)} %collective-permute-done.1.block_ref), custom_call_target="tpu_custom_call" | custom-call | flops 1048576 | bytes 1048576 | tf_op jit(solution)/shard_map/pallas_call | solution.py:112
  28.8 16.2 %all-to-all-start.1 = ((bf16[32,48,128]{2,1,0:T(8,128)(2,1)}), bf16[32,48,128]{2,1,0:T(8,128)(2,1)S(1)}, u32[]{:S(2)}, u32[]{:S(2)}) async-start(bf16[32,48,128]{2,1,0:T(8,128)(2,1)} %shard_map.76), calls=%async_computation.1 | async-start | bytes 786432 | tf_op jit(solution)/shard_map/all_to_all | solution.py:330
  45.0 2.4 %collective-permute-start.2 = (bf16[256,2176]{1,0:T(8,128)(2,1)S(1)}, bf16[256,2176]{1,0:T(8,128)(2,1)S(1)}, u32[]{:S(2)}, u32[]{:S(2)}) collective-permute-start(bf16[256,2176]{1,0:T(8,128)(2,1)S(1)} %bitcast.14), channel_id=1, source_target_pairs={{0,1},{1,0},{2,3},{3,2},{4,5},{5,4},{6,7},{7,6},{8,9},{9,8},{10,11... | collective-permute-start | bytes 3342344 | tf_op jit(solution)/shard_map/ppermute | solution.py:333
  47.4 12.3 %all-to-all-done.1.parts_ref = bf16[32,48,128]{2,1,0:T(8,128)(2,1)S(1)} async-done(((bf16[32,48,128]{2,1,0:T(8,128)(2,1)}), bf16[32,48,128]{2,1,0:T(8,128)(2,1)S(1)}, u32[]{:S(2)}, u32[]{:S(2)}) %all-to-all-start.1) | async-done | bytes 393248 | tf_op jit(solution)/shard_map/all_to_all | solution.py:330
  59.7 0.9 shard_map.77
  60.6 6.6 %all-to-all-start.2 = ((f32[8,32,128]{2,1,0:T(8,128)}), f32[8,32,128]{2,1,0:T(8,128)S(1)}, u32[]{:S(2)}, u32[]{:S(2)}) async-start(f32[8,32,128]{2,1,0:T(8,128)} %shard_map.77), calls=%async_computation.2 | async-start | bytes 262144 | tf_op jit(solution)/shard_map/all_to_all | solution.py:335
  67.2 0.0 copy-done.1
  67.2 0.0 copy-done.2
  67.2 0.8 shard_map.74
  68.0 4.5 %all-to-all-done.2.pieces_ref = f32[8,32,128]{2,1,0:T(8,128)S(1)} async-done(((f32[8,32,128]{2,1,0:T(8,128)}), f32[8,32,128]{2,1,0:T(8,128)S(1)}, u32[]{:S(2)}, u32[]{:S(2)}) %all-to-all-start.2) | async-done | bytes 131104 | tf_op jit(solution)/shard_map/all_to_all | solution.py:335
  72.5 3.4 %shard_map.78 = bf16[32,2,8,128]{3,2,1,0:T(8,128)(2,1)S(1)} custom-call(bf16[1024,128]{1,0:T(8,128)(2,1)S(1)} %get-tuple-element.10.runs_ref, bf16[4,128,512]{2,1,0:T(8,128)(2,1)S(1)} %get-tuple-element.11.new_ref, f32[8,32,128]{2,1,0:T(8,128)S(1)} %all-to-all-done.2.pieces_ref, f32[8,128]{1,0:T(8,128)S(1)} %get-tuple-element.14.aux_ref), custom_call_target="tpu_custom_call" | custom-call | flops 268435456 | bytes 1048576 | tf_op jit(solution)/shard_map/pallas_call | solution.py:248
  75.9 16.8 %all_to_all.20 = bf16[64,8,128]{2,1,0:T(8,128)(2,1)S(1)} all-to-all(bf16[64,8,128]{2,1,0:T(8,128)(2,1)S(1)} %bitcast.19), channel_id=1, replica_groups=mesh['zh'=4,'y'=8,'core'=2,'x'=4,'zl'=2] {'zh','y','zl'}, dimensions={0} | all-to-all | bytes 262144 | tf_op jit(solution)/shard_map/all_to_all | solution.py:337
  92.7 3.9 %all_gather.11 = bf16[128,8,128]{2,1,0:T(8,128)(2,1)S(1)} all-gather(bf16[64,8,128]{2,1,0:T(8,128)(2,1)S(1)} %all_to_all.20), channel_id=1, replica_groups=mesh['zh'=4,'y'=8,'core'=2,'x'=4,'zl'=2] {'core'}, dimensions={0}, use_global_device_ids=true | all-gather | bytes 393216 | tf_op jit(solution)/shard_map/all_gather | solution.py:338
  96.6 0.0 collective-permute-done.2.refs_3_
  96.6 2.1 %shard_map.79 = bf16[256,2048]{1,0:T(8,128)(2,1)} custom-call(s32[5]{0:T(128)S(1)} %stack.23.where_ref.refs_0_, bf16[64,2,8,128]{3,2,1,0:T(8,128)(2,1)S(1)} %bitcast.18, bf16[256,2176]{1,0:T(8,128)(2,1)S(1)} %bitcast.16, bf16[256,2176]{1,0:T(8,128)(2,1)S(1)} %collective-permute-done.2.refs_3_), custom_call_target="tpu_custom_call" | custom-call | flops 536870912 | bytes 3145728 | tf_op jit(solution)/shard_map/pallas_call | solution.py:296
  (1 shorter events, 0.0 us)
Async XLA Ops:
  2.1 5.0 %copy-start = (bf16[128,2048]{1,0:T(8,128)(2,1)S(1)}, bf16[128,2048]{1,0:T(8,128)(2,1)}, u32[]{:S(2)}) copy-start(bf16[128,2048]{1,0:T(8,128)(2,1)} %refs_1_.1) | copy-start | bytes 1572868
  2.1 9.0 %copy-start.3 = (f32[1024,16]{0,1:T(8,128)S(1)}, f32[1024,16]{0,1:T(8,128)}, u32[]{:S(2)}) copy-start(f32[1024,16]{0,1:T(8,128)} %param.9) | copy-start | bytes 196612
  2.1 16.9 %all-to-all-start = ((bf16[4,64,2176]{2,1,0:T(8,128)(2,1)}), bf16[4,64,2176]{2,1,0:T(8,128)(2,1)S(1)}, u32[]{:S(2)}, u32[]{:S(2)}) async-start(bf16[4,64,2176]{2,1,0:T(8,128)(2,1)} %shard_map.73), calls=%async_computation | async-start | bytes 2228224 | tf_op jit(solution)/shard_map/all_to_all | solution.py:319
  7.0 12.0 %collective-permute-start = (bf16[128,2048]{1,0:T(8,128)(2,1)S(1)}, bf16[128,2048]{1,0:T(8,128)(2,1)S(1)}, u32[]{:S(2)}, u32[]{:S(2)}) collective-permute-start(bf16[128,2048]{1,0:T(8,128)(2,1)S(1)} %copy-done), channel_id=1, source_target_pairs={{0,1},{1,0},{2,3},{3,2},{4,5},{5,4},{6,7},{7,6},{8,9},{9,8},{10,11... | collective-permute-start | bytes 1572872 | tf_op jit(solution)/shard_map/ppermute | solution.py:318
  11.1 16.3 %collective-permute-start.1 = (bf16[16,1024]{1,0:T(8,128)(2,1)S(1)}, bf16[16,1024]{1,0:T(8,128)(2,1)S(1)}, u32[]{:S(2)}, u32[]{:S(2)}) collective-permute-start(bf16[16,1024]{1,0:T(8,128)(2,1)S(1)} %convert_bitcast_fusion), channel_id=1, source_target_pairs={{0,0},{2,128},{4,256},{6,384},{128,2},{130,130},{132,258},{134,386... | collective-permute-start | bytes 98312 | tf_op jit(solution)/shard_map/ppermute | solution.py:322
  27.3 39.9 %copy-start.1 = (f32[8,2048]{1,0:T(8,128)S(1)}, f32[8,2048]{1,0:T(8,128)}, u32[]{:S(2)}) copy-start(f32[8,2048]{1,0:T(8,128)} %new_ref.1) | copy-start | bytes 196612
  27.3 39.9 %copy-start.2 = (f32[8,1024]{1,0:T(8,128)S(1)}, f32[8,1024]{1,0:T(8,128)}, u32[]{:S(2)}) copy-start(f32[8,1024]{1,0:T(8,128)} %design_ref.1) | copy-start | bytes 98308
  28.8 30.9 %all-to-all-start.1 = ((bf16[32,48,128]{2,1,0:T(8,128)(2,1)}), bf16[32,48,128]{2,1,0:T(8,128)(2,1)S(1)}, u32[]{:S(2)}, u32[]{:S(2)}) async-start(bf16[32,48,128]{2,1,0:T(8,128)(2,1)} %shard_map.76), calls=%async_computation.1 | async-start | bytes 786432 | tf_op jit(solution)/shard_map/all_to_all | solution.py:330
  45.0 51.6 %collective-permute-start.2 = (bf16[256,2176]{1,0:T(8,128)(2,1)S(1)}, bf16[256,2176]{1,0:T(8,128)(2,1)S(1)}, u32[]{:S(2)}, u32[]{:S(2)}) collective-permute-start(bf16[256,2176]{1,0:T(8,128)(2,1)S(1)} %bitcast.14), channel_id=1, source_target_pairs={{0,1},{1,0},{2,3},{3,2},{4,5},{5,4},{6,7},{7,6},{8,9},{9,8},{10,11... | collective-permute-start | bytes 3342344 | tf_op jit(solution)/shard_map/ppermute | solution.py:333
  60.6 11.9 %all-to-all-start.2 = ((f32[8,32,128]{2,1,0:T(8,128)}), f32[8,32,128]{2,1,0:T(8,128)S(1)}, u32[]{:S(2)}, u32[]{:S(2)}) async-start(f32[8,32,128]{2,1,0:T(8,128)} %shard_map.77), calls=%async_computation.2 | async-start | bytes 262144 | tf_op jit(solution)/shard_map/all_to_all | solution.py:335

commit v5 on v4

--- a/solution.py
+++ b/solution.py
@@ -120,7 +120,7 @@
     )(where, mine, theirs, block)
 
 
-def weights_kernel(parts_ref, out_ref, winv_ref):
+def weights_kernel(parts_ref, after_ref, out_ref, winv_ref):
     for chip in range(32):
         zh, y = chip // 8, chip % 8
         for side in range(2):
@@ -143,16 +143,16 @@
                     out_ref[2 * peer + core, row : row + 1, :] = piece
 
 
-def weights(parts):
+def weights(parts, after):
     return pl.pallas_call(
         weights_kernel,
         out_shape=jax.ShapeDtypeStruct((8, 32, 128), F32),
-        in_specs=[VMEM],
+        in_specs=[VMEM, pl.BlockSpec(memory_space=pl.ANY)],
         out_specs=VMEM,
         scratch_shapes=[pltpu.VMEM((128, 1024), BF16)],
         compiler_params=params(16),
         cost_estimate=pl.CostEstimate(flops=1 << 23, bytes_accessed=1 << 20, transcendentals=0),
-    )(parts)
+    )(parts, after)
 
 
 def prepare_kernel(where_ref, side_ref, design_ref, new_ref, runs_ref, new_out_ref, aux_ref, wide_ref):
@@ -214,13 +214,14 @@
 def predict_kernel(runs_ref, new_ref, pieces_ref, aux_ref, out_ref, spread_ref, pred_ref):
     both = jnp.sum(pieces_ref[...], axis=0)
     parts = [p.astype(F32) for p in split3(both)]
-    table = jnp.concatenate(parts + [jnp.zeros((32, 128), F32)], axis=0).T.astype(BF16)
+    table = jnp.concatenate(parts + [jnp.zeros((32, 128), F32)], axis=0).T
     row = lax.broadcasted_iota(jnp.int32, (128, 512), 0)
     col = lax.broadcasted_iota(jnp.int32, (128, 512), 1)
+    pick = ((row % 32 == 8 * (col // 128)) & (row < 96)).astype(BF16)
     for tile in range(8):
-        pick = ((row % 32 == 8 * (col // 128) + tile) & (row < 96)).astype(BF16)
+        rolled = pltpu.roll(table, (128 - tile) % 128, axis=1).astype(BF16)
         spread_ref[128 * tile : 128 * tile + 128, :] = jnp.dot(
-            table, pick, preferred_element_type=F32
+            rolled, pick, preferred_element_type=F32
         )
 
     for block in range(4):
@@ -332,7 +333,7 @@
     runs_feat, new_feat, aux = prepare(where, basis, design, new_settings)
     basis_other = lax.ppermute(basis, "zl", swap)
 
-    pieces = lax.all_to_all(weights(parts), ("x", "core"), 0, 0, tiled=True)
+    pieces = lax.all_to_all(weights(parts, aux), ("x", "core"), 0, 0, tiled=True)
     pred = predict(runs_feat, new_feat, pieces, aux)
     pred = lax.all_to_all(pred.reshape(64, 8, 128), ("zh", "y", "zl"), 0, 0, tiled=True)
     pred = lax.all_gather(pred, "core", axis=0, tiled=True)

time: 99.2 us -> 98.6 us (level)
  blocking collectives: 27.9 us -> 39.8 us
  starting transfers between devices: 34.9 us -> 28.3 us
  waiting for transfers between devices: 23.9 us -> 18.6 us
    all_to_all x0 -> x1, blocking collectives: none -> 11.7 us  [on_device(): lax.all_to_all(weights(parts, aux), ('x', 'core'), 0, 0, tiled=True)]
    all_to_all x1 -> x0, starting transfers between devices: 6.61 us -> none  [on_device(): pieces = lax.all_to_all(weights(parts), ('x', 'core'), 0, 0, tiled=True)]
    all_to_all x1 -> x0, waiting for transfers between devices: 4.48 us -> none  [on_device(): pieces = lax.all_to_all(weights(parts), ('x', 'core'), 0, 0, tiled=True)]
  transfers between devices with their start and end apart: 6 -> 5, of which waited for: 3 -> 2; matrix products, arithmetic and copies ran while one was open for 0% -> 0% of each run, Pallas kernels for 6% -> 6%
where the time goes in v5:
time: 98.6 us; the launch traced here: 98.1 us
  blocking collectives  39.8 us (40%)
  starting transfers between devices  28.3 us (29%)
  waiting for transfers between devices  18.6 us (19%)
  Pallas kernels  11.2 us (11%)
    all_to_all x1, blocking collectives, on_device(): lax.all_to_all(pred.reshape(64, 8, 128), ('zh', 'y', 'zl'), 0, 0, tiled=T...  16.8 us
    all_to_all x1, starting transfers between devices, on_device(): lax.all_to_all(slots(where, mine, theirs, block), ('zh', 'y'), 0, 0, tile...  16.2 us
    all_to_all x1, blocking collectives, on_device(): lax.all_to_all(weights(parts, aux), ('x', 'core'), 0, 0, tiled=True)  11.7 us
    all_to_all x1, waiting for transfers between devices, on_device(): lax.all_to_all(slots(where, mine, theirs, block), ('zh', 'y'), 0, 0, tile...  11.5 us
    all_gather x1, blocking collectives, on_device(): theirs = lax.all_gather(theirs, 'core', axis=0)  7.36 us
    ppermute x1, waiting for transfers between devices, on_device(): fields_other = lax.ppermute(fields_runs, 'zl', swap)  7.18 us
    all_to_all x1, starting transfers between devices, on_device(): lax.all_to_all(pack(eof_basis.T, lscale, variance.reshape(1, 64)), 'x', 0...  4.97 us
    ppermute x1, starting transfers between devices, on_device(): fields_other = lax.ppermute(fields_runs, 'zl', swap)  3.99 us
  transfers between devices with their start and end apart: 5, of which 2 were waited for; matrix products, arithmetic and copies ran while one was open for 0% of the time, Pallas kernels for 6%

profile of v5, /device:TPU:1, one launch (start us, length us, event | category | flops | bytes accessed | tf_op | source)
XLA Modules:
  0.0 98.1 jit_solution(1578078835591899362)
XLA Ops:
  0.0 2.1 %shard_map.73 = bf16[4,64,2176]{2,1,0:T(8,128)(2,1)} custom-call(bf16[64,2048]{1,0:T(8,128)(2,1)} %bitcast.20, f32[8,64]{1,0:T(8,128)} %lscale_ref.1, f32[1,64]{1,0:T(1,128)} %bitcast.21), custom_call_target="tpu_custom_call" | custom-call | bytes 1310720 | tf_op jit(solution)/shard_map/pallas_call | solution.py:49
  2.1 0.0 copy-start
  2.1 0.0 copy-start.3
  2.1 5.0 %all-to-all-start = ((bf16[4,64,2176]{2,1,0:T(8,128)(2,1)}), bf16[4,64,2176]{2,1,0:T(8,128)(2,1)S(1)}, u32[]{:S(2)}, u32[]{:S(2)}) async-start(bf16[4,64,2176]{2,1,0:T(8,128)(2,1)} %shard_map.73), calls=%async_computation | async-start | bytes 2228224 | tf_op jit(solution)/shard_map/all_to_all | solution.py:320
  7.0 0.0 copy-done
  7.0 4.0 %collective-permute-start = (bf16[128,2048]{1,0:T(8,128)(2,1)S(1)}, bf16[128,2048]{1,0:T(8,128)(2,1)S(1)}, u32[]{:S(2)}, u32[]{:S(2)}) collective-permute-start(bf16[128,2048]{1,0:T(8,128)(2,1)S(1)} %copy-done), channel_id=1, source_target_pairs={{0,1},{1,0},{2,3},{3,2},{4,5},{5,4},{6,7},{7,6},{8,9},{9,8},{10,11... | collective-permute-start | bytes 1572872 | tf_op jit(solution)/shard_map/ppermute | solution.py:319
  11.0 0.0 copy-done.3
  11.1 0.7 collective-permute-start.1
  11.7 0.1 stack.23.where_ref.refs_0_
  11.8 7.2 %collective-permute-done.refs_2_ = bf16[128,2048]{1,0:T(8,128)(2,1)S(1)} collective-permute-done((bf16[128,2048]{1,0:T(8,128)(2,1)S(1)}, bf16[128,2048]{1,0:T(8,128)(2,1)S(1)}, u32[]{:S(2)}, u32[]{:S(2)}) %collective-permute-start) | collective-permute-done | bytes 524320 | tf_op jit(solution)/shard_map/ppermute | solution.py:319
  19.0 0.0 all-to-all-done
  19.0 1.1 %shard_map.75 = (f32[256,128]{1,0:T(8,128)S(1)}, f32[256,128]{1,0:T(8,128)S(1)}) custom-call(s32[5]{0:T(128)S(1)} %stack.23.where_ref.refs_0_, bf16[128,2048]{1,0:T(8,128)(2,1)S(1)} %copy-done, bf16[128,2048]{1,0:T(8,128)(2,1)S(1)} %collective-permute-done.refs_2_, bf16[256,2176]{1,0:T(8,128)(2,1)S(1)} %bitcast.13), custom_call_target="tpu_custom_call" | custom-call | flops 268435456 | bytes 2097152 | tf_op jit(solution)/shard_map/pallas_call | solution.py:82
  20.1 0.0 copy-start.1
  20.1 0.0 copy-start.2
  20.1 7.4 %all-gather = f32[512,128]{1,0:T(8,128)S(1)} all-gather(f32[256,128]{1,0:T(8,128)S(1)} %get-tuple-element.13), channel_id=2, replica_groups=mesh['zh'=4,'y'=8,'core'=2,'x'=4,'zl'=2] {'core'}, dimensions={0}, use_global_device_ids=true | all-gather | bytes 393216 | tf_op jit(solution)/shard_map/all_gather | solution.py:330
  27.5 0.0 collective-permute-done.1.block_ref
  27.5 1.4 %shard_map.76 = bf16[32,48,128]{2,1,0:T(8,128)(2,1)} custom-call(s32[5]{0:T(128)S(1)} %stack.23.where_ref.refs_0_, f32[256,128]{1,0:T(8,128)S(1)} %get-tuple-element.12.mine_ref, f32[2,256,128]{2,1,0:T(8,128)S(1)} %bitcast.17, bf16[16,1024]{1,0:T(8,128)(2,1)S(1)} %collective-permute-done.1.block_ref), custom_call_target="tpu_custom_call" | custom-call | flops 1048576 | bytes 1048576 | tf_op jit(solution)/shard_map/pallas_call | solution.py:112
  28.9 16.2 %all-to-all-start.1 = ((bf16[32,48,128]{2,1,0:T(8,128)(2,1)}), bf16[32,48,128]{2,1,0:T(8,128)(2,1)S(1)}, u32[]{:S(2)}, u32[]{:S(2)}) async-start(bf16[32,48,128]{2,1,0:T(8,128)(2,1)} %shard_map.76), calls=%async_computation.1 | async-start | bytes 786432 | tf_op jit(solution)/shard_map/all_to_all | solution.py:331
  45.2 2.4 %collective-permute-start.2 = (bf16[256,2176]{1,0:T(8,128)(2,1)S(1)}, bf16[256,2176]{1,0:T(8,128)(2,1)S(1)}, u32[]{:S(2)}, u32[]{:S(2)}) collective-permute-start(bf16[256,2176]{1,0:T(8,128)(2,1)S(1)} %bitcast.14), channel_id=1, source_target_pairs={{0,1},{1,0},{2,3},{3,2},{4,5},{5,4},{6,7},{7,6},{8,9},{9,8},{10,11... | collective-permute-start | bytes 3342344 | tf_op jit(solution)/shard_map/ppermute | solution.py:334
  47.6 0.0 copy-done.1
  47.6 0.0 copy-done.2
  47.6 0.8 shard_map.74
  48.4 11.5 %all-to-all-done.1.parts_ref = bf16[32,48,128]{2,1,0:T(8,128)(2,1)S(1)} async-done(((bf16[32,48,128]{2,1,0:T(8,128)(2,1)}), bf16[32,48,128]{2,1,0:T(8,128)(2,1)S(1)}, u32[]{:S(2)}, u32[]{:S(2)}) %all-to-all-start.1) | async-done | bytes 393248 | tf_op jit(solution)/shard_map/all_to_all | solution.py:331
  59.9 0.2 shard_map.77
  60.1 11.7 %all_to_all.20.pieces_ref = f32[8,32,128]{2,1,0:T(8,128)S(1)} all-to-all(f32[8,32,128]{2,1,0:T(8,128)S(1)} %shard_map.77), channel_id=1, replica_groups=mesh['zh'=4,'y'=8,'core'=2,'x'=4,'zl'=2] {'x','core'}, dimensions={0} | all-to-all | bytes 262144 | tf_op jit(solution)/shard_map/all_to_all | solution.py:336
  71.8 3.5 %shard_map.78 = bf16[32,2,8,128]{3,2,1,0:T(8,128)(2,1)S(1)} custom-call(bf16[1024,128]{1,0:T(8,128)(2,1)S(1)} %get-tuple-element.10.runs_ref, bf16[4,128,512]{2,1,0:T(8,128)(2,1)S(1)} %get-tuple-element.11.new_ref, f32[8,32,128]{2,1,0:T(8,128)S(1)} %all_to_all.20.pieces_ref, f32[8,128]{1,0:T(8,128)S(1)} %get-tuple-element.14.after_ref.aux_ref), custom_call_target="tpu_custom_call" | custom-call | flops 268435456 | bytes 1048576 | tf_op jit(solution)/shard_map/pallas_call | solution.py:249
  75.3 16.8 %all_to_all.21 = bf16[64,8,128]{2,1,0:T(8,128)(2,1)S(1)} all-to-all(bf16[64,8,128]{2,1,0:T(8,128)(2,1)S(1)} %bitcast.19), channel_id=1, replica_groups=mesh['zh'=4,'y'=8,'core'=2,'x'=4,'zl'=2] {'zh','y','zl'}, dimensions={0} | all-to-all | bytes 262144 | tf_op jit(solution)/shard_map/all_to_all | solution.py:338
  92.1 3.9 %all_gather.11 = bf16[128,8,128]{2,1,0:T(8,128)(2,1)S(1)} all-gather(bf16[64,8,128]{2,1,0:T(8,128)(2,1)S(1)} %all_to_all.21), channel_id=1, replica_groups=mesh['zh'=4,'y'=8,'core'=2,'x'=4,'zl'=2] {'core'}, dimensions={0}, use_global_device_ids=true | all-gather | bytes 393216 | tf_op jit(solution)/shard_map/all_gather | solution.py:339
  96.0 0.0 collective-permute-done.2.refs_3_
  96.0 2.1 %shard_map.79 = bf16[256,2048]{1,0:T(8,128)(2,1)} custom-call(s32[5]{0:T(128)S(1)} %stack.23.where_ref.refs_0_, bf16[64,2,8,128]{3,2,1,0:T(8,128)(2,1)S(1)} %bitcast.18, bf16[256,2176]{1,0:T(8,128)(2,1)S(1)} %bitcast.16, bf16[256,2176]{1,0:T(8,128)(2,1)S(1)} %collective-permute-done.2.refs_3_), custom_call_target="tpu_custom_call" | custom-call | flops 536870912 | bytes 3145728 | tf_op jit(solution)/shard_map/pallas_call | solution.py:297
  (1 shorter events, 0.0 us)
Async XLA Ops:
  2.1 5.0 %copy-start = (bf16[128,2048]{1,0:T(8,128)(2,1)S(1)}, bf16[128,2048]{1,0:T(8,128)(2,1)}, u32[]{:S(2)}) copy-start(bf16[128,2048]{1,0:T(8,128)(2,1)} %refs_1_.1) | copy-start | bytes 1572868
  2.1 9.0 %copy-start.3 = (f32[1024,16]{0,1:T(8,128)S(1)}, f32[1024,16]{0,1:T(8,128)}, u32[]{:S(2)}) copy-start(f32[1024,16]{0,1:T(8,128)} %param.9) | copy-start | bytes 196612
  2.1 16.9 %all-to-all-start = ((bf16[4,64,2176]{2,1,0:T(8,128)(2,1)}), bf16[4,64,2176]{2,1,0:T(8,128)(2,1)S(1)}, u32[]{:S(2)}, u32[]{:S(2)}) async-start(bf16[4,64,2176]{2,1,0:T(8,128)(2,1)} %shard_map.73), calls=%async_computation | async-start | bytes 2228224 | tf_op jit(solution)/shard_map/all_to_all | solution.py:320
  7.0 12.0 %collective-permute-start = (bf16[128,2048]{1,0:T(8,128)(2,1)S(1)}, bf16[128,2048]{1,0:T(8,128)(2,1)S(1)}, u32[]{:S(2)}, u32[]{:S(2)}) collective-permute-start(bf16[128,2048]{1,0:T(8,128)(2,1)S(1)} %copy-done), channel_id=1, source_target_pairs={{0,1},{1,0},{2,3},{3,2},{4,5},{5,4},{6,7},{7,6},{8,9},{9,8},{10,11... | collective-permute-start | bytes 1572872 | tf_op jit(solution)/shard_map/ppermute | solution.py:319
  11.1 16.4 %collective-permute-start.1 = (bf16[16,1024]{1,0:T(8,128)(2,1)S(1)}, bf16[16,1024]{1,0:T(8,128)(2,1)S(1)}, u32[]{:S(2)}, u32[]{:S(2)}) collective-permute-start(bf16[16,1024]{1,0:T(8,128)(2,1)S(1)} %convert_bitcast_fusion), channel_id=1, source_target_pairs={{0,0},{2,128},{4,256},{6,384},{128,2},{130,130},{132,258},{134,386... | collective-permute-start | bytes 98312 | tf_op jit(solution)/shard_map/ppermute | solution.py:323
  20.1 27.5 %copy-start.1 = (f32[8,2048]{1,0:T(8,128)S(1)}, f32[8,2048]{1,0:T(8,128)}, u32[]{:S(2)}) copy-start(f32[8,2048]{1,0:T(8,128)} %new_ref.1) | copy-start | bytes 196612
  20.1 27.5 %copy-start.2 = (f32[8,1024]{1,0:T(8,128)S(1)}, f32[8,1024]{1,0:T(8,128)}, u32[]{:S(2)}) copy-start(f32[8,1024]{1,0:T(8,128)} %design_ref.1) | copy-start | bytes 98308
  28.9 30.9 %all-to-all-start.1 = ((bf16[32,48,128]{2,1,0:T(8,128)(2,1)}), bf16[32,48,128]{2,1,0:T(8,128)(2,1)S(1)}, u32[]{:S(2)}, u32[]{:S(2)}) async-start(bf16[32,48,128]{2,1,0:T(8,128)(2,1)} %shard_map.76), calls=%async_computation.1 | async-start | bytes 786432 | tf_op jit(solution)/shard_map/all_to_all | solution.py:331
  45.2 50.8 %collective-permute-start.2 = (bf16[256,2176]{1,0:T(8,128)(2,1)S(1)}, bf16[256,2176]{1,0:T(8,128)(2,1)S(1)}, u32[]{:S(2)}, u32[]{:S(2)}) collective-permute-start(bf16[256,2176]{1,0:T(8,128)(2,1)S(1)} %bitcast.14), channel_id=1, source_target_pairs={{0,1},{1,0},{2,3},{3,2},{4,5},{5,4},{6,7},{7,6},{8,9},{9,8},{10,11... | collective-permute-start | bytes 3342344 | tf_op jit(solution)/shard_map/ppermute | solution.py:334

commit v6 on v5

--- a/solution.py
+++ b/solution.py
@@ -18,6 +18,7 @@
 SMEM = pl.BlockSpec(memory_space=pltpu.SMEM)
 CELLS = 2048
 WIDE = CELLS + 128
+BOUNDS = (0, 768, 1280, 1792, 2048)
 
 
 def params(mib):
@@ -90,7 +91,14 @@
     )(where, own, other, basis)
 
 
-def slots_kernel(where_ref, mine_ref, theirs_ref, block_ref, out_ref, wide_ref):
+def slots_kernel(where_ref, mine_ref, theirs_ref, block_ref, out_ref, held_ref, wide_ref, sems):
+    for side in range(2):
+        lanes = pl.ds(pl.multiple_of(256 * where_ref[3] + 128 * side, 128), 128)
+        piece = block_ref[:, lanes]
+        for chip in range(32):
+            held_ref[chip, 16 + 16 * side : 32 + 16 * side, :] = piece
+    lower = pltpu.make_async_copy(held_ref.at[:, 16:, :], out_ref.at[:, 16:, :], sems.at[0])
+    lower.start()
     part = mine_ref[...] + theirs_ref[1 - where_ref[4]]
     high = part.astype(BF16).astype(F32)
     low = part - high
@@ -100,12 +108,11 @@
             row = 4 * core + block
             wide_ref[pl.ds(row, 32, stride=16), :] = high[first : first + 32]
             wide_ref[pl.ds(row + 8, 32, stride=16), :] = low[first : first + 32]
-    out_ref[:, :16, :] = wide_ref[...].astype(BF16).reshape(32, 16, 128)
-    for side in range(2):
-        lanes = pl.ds(pl.multiple_of(256 * where_ref[3] + 128 * side, 128), 128)
-        piece = block_ref[:, lanes]
-        for chip in range(32):
-            out_ref[chip, 16 + 16 * side : 32 + 16 * side, :] = piece
+    held_ref[:, :16, :] = wide_ref[...].astype(BF16).reshape(32, 16, 128)
+    upper = pltpu.make_async_copy(held_ref.at[:, :16, :], out_ref.at[:, :16, :], sems.at[1])
+    upper.start()
+    lower.wait()
+    upper.wait()
 
 
 def slots(where, mine, theirs, block):
@@ -113,8 +120,12 @@
         slots_kernel,
         out_shape=jax.ShapeDtypeStruct((32, 48, 128), BF16),
         in_specs=[SMEM] + [VMEM] * 3,
-        out_specs=VMEM,
-        scratch_shapes=[pltpu.VMEM((512, 128), F32)],
+        out_specs=pl.BlockSpec(memory_space=pl.ANY),
+        scratch_shapes=[
+            pltpu.VMEM((32, 48, 128), BF16),
+            pltpu.VMEM((512, 128), F32),
+            pltpu.SemaphoreType.DMA((2,)),
+        ],
         compiler_params=params(16),
         cost_estimate=pl.CostEstimate(flops=1 << 20, bytes_accessed=1 << 20, transcendentals=0),
     )(where, mine, theirs, block)
@@ -279,7 +290,7 @@
 
     copies = []
     for chunk in range(4):
-        cells = slice(512 * chunk, 512 * chunk + 512)
+        cells = slice(BOUNDS[chunk], BOUNDS[chunk + 1])
         total = jnp.dot(lhs_ref[:, :256], own_ref[:, cells], preferred_element_type=F32)
         total = total + jnp.dot(lhs_ref[:, 256:], other_ref[:, cells], preferred_element_type=F32)
         done_ref[:, cells] = (total * scale).astype(BF16)

time: 98.6 us -> 98.5 us (level)
  no operation moved by 1% of the time
where the time goes in v6:
time: 98.5 us; the launch traced here: 98.1 us
  blocking collectives  39.7 us (40%)
  starting transfers between devices  28.3 us (29%)
  waiting for transfers between devices  18.6 us (19%)
  Pallas kernels  11.2 us (11%)
    all_to_all x1, blocking collectives, on_device(): lax.all_to_all(pred.reshape(64, 8, 128), ('zh', 'y', 'zl'), 0, 0, tiled=T...  16.8 us
    all_to_all x1, starting transfers between devices, on_device(): lax.all_to_all(slots(where, mine, theirs, block), ('zh', 'y'), 0, 0, tile...  16.3 us
    all_to_all x1, blocking collectives, on_device(): lax.all_to_all(weights(parts, aux), ('x', 'core'), 0, 0, tiled=True)  11.7 us
    all_to_all x1, waiting for transfers between devices, on_device(): lax.all_to_all(slots(where, mine, theirs, block), ('zh', 'y'), 0, 0, tile...  11.5 us
    all_gather x1, blocking collectives, on_device(): theirs = lax.all_gather(theirs, 'core', axis=0)  7.36 us
    ppermute x1, waiting for transfers between devices, on_device(): fields_other = lax.ppermute(fields_runs, 'zl', swap)  7.18 us
    all_to_all x1, starting transfers between devices, on_device(): lax.all_to_all(pack(eof_basis.T, lscale, variance.reshape(1, 64)), 'x', 0...  4.97 us
    ppermute x1, starting transfers between devices, on_device(): fields_other = lax.ppermute(fields_runs, 'zl', swap)  3.99 us
  transfers between devices with their start and end apart: 5, of which 2 were waited for; matrix products, arithmetic and copies ran while one was open for 0% of the time, Pallas kernels for 6%

profile of v6, /device:TPU:1, one launch (start us, length us, event | category | flops | bytes accessed | tf_op | source)
XLA Modules:
  0.0 98.1 jit_solution(15492496262818615726)
XLA Ops:
  0.0 2.1 %shard_map.73 = bf16[4,64,2176]{2,1,0:T(8,128)(2,1)} custom-call(bf16[64,2048]{1,0:T(8,128)(2,1)} %bitcast.20, f32[8,64]{1,0:T(8,128)} %lscale_ref.1, f32[1,64]{1,0:T(1,128)} %bitcast.21), custom_call_target="tpu_custom_call" | custom-call | bytes 1310720 | tf_op jit(solution)/shard_map/pallas_call | solution.py:50
  2.1 0.0 copy-start
  2.1 0.0 copy-start.3
  2.1 5.0 %all-to-all-start = ((bf16[4,64,2176]{2,1,0:T(8,128)(2,1)}), bf16[4,64,2176]{2,1,0:T(8,128)(2,1)S(1)}, u32[]{:S(2)}, u32[]{:S(2)}) async-start(bf16[4,64,2176]{2,1,0:T(8,128)(2,1)} %shard_map.73), calls=%async_computation | async-start | bytes 2228224 | tf_op jit(solution)/shard_map/all_to_all | solution.py:331
  7.0 0.0 copy-done
  7.0 4.0 %collective-permute-start = (bf16[128,2048]{1,0:T(8,128)(2,1)S(1)}, bf16[128,2048]{1,0:T(8,128)(2,1)S(1)}, u32[]{:S(2)}, u32[]{:S(2)}) collective-permute-start(bf16[128,2048]{1,0:T(8,128)(2,1)S(1)} %copy-done), channel_id=1, source_target_pairs={{0,1},{1,0},{2,3},{3,2},{4,5},{5,4},{6,7},{7,6},{8,9},{9,8},{10,11... | collective-permute-start | bytes 1572872 | tf_op jit(solution)/shard_map/ppermute | solution.py:330
  11.0 0.0 copy-done.3
  11.1 0.7 collective-permute-start.1
  11.7 0.1 stack.23.where_ref.refs_0_
  11.8 7.2 %collective-permute-done.refs_2_ = bf16[128,2048]{1,0:T(8,128)(2,1)S(1)} collective-permute-done((bf16[128,2048]{1,0:T(8,128)(2,1)S(1)}, bf16[128,2048]{1,0:T(8,128)(2,1)S(1)}, u32[]{:S(2)}, u32[]{:S(2)}) %collective-permute-start) | collective-permute-done | bytes 524320 | tf_op jit(solution)/shard_map/ppermute | solution.py:330
  19.0 0.0 all-to-all-done
  19.0 1.1 %shard_map.75 = (f32[256,128]{1,0:T(8,128)S(1)}, f32[256,128]{1,0:T(8,128)S(1)}) custom-call(s32[5]{0:T(128)S(1)} %stack.23.where_ref.refs_0_, bf16[128,2048]{1,0:T(8,128)(2,1)S(1)} %copy-done, bf16[128,2048]{1,0:T(8,128)(2,1)S(1)} %collective-permute-done.refs_2_, bf16[256,2176]{1,0:T(8,128)(2,1)S(1)} %bitcast.13), custom_call_target="tpu_custom_call" | custom-call | flops 268435456 | bytes 2097152 | tf_op jit(solution)/shard_map/pallas_call | solution.py:83
  20.1 0.0 copy-start.1
  20.1 0.0 copy-start.2
  20.1 7.4 %all-gather = f32[512,128]{1,0:T(8,128)S(1)} all-gather(f32[256,128]{1,0:T(8,128)S(1)} %get-tuple-element.13), channel_id=2, replica_groups=mesh['zh'=4,'y'=8,'core'=2,'x'=4,'zl'=2] {'core'}, dimensions={0}, use_global_device_ids=true | all-gather | bytes 393216 | tf_op jit(solution)/shard_map/all_gather | solution.py:341
  27.5 0.0 collective-permute-done.1.block_ref
  27.5 1.4 %shard_map.76 = bf16[32,48,128]{2,1,0:T(8,128)(2,1)} custom-call(s32[5]{0:T(128)S(1)} %stack.23.where_ref.refs_0_, f32[256,128]{1,0:T(8,128)S(1)} %get-tuple-element.12.mine_ref, f32[2,256,128]{2,1,0:T(8,128)S(1)} %bitcast.17, bf16[16,1024]{1,0:T(8,128)(2,1)S(1)} %collective-permute-done.1.block_ref), custom_call_target="tpu_custom_call" | custom-call | flops 1048576 | bytes 1048576 | tf_op jit(solution)/shard_map/pallas_call | solution.py:119
  28.9 16.3 %all-to-all-start.1 = ((bf16[32,48,128]{2,1,0:T(8,128)(2,1)}), bf16[32,48,128]{2,1,0:T(8,128)(2,1)S(1)}, u32[]{:S(2)}, u32[]{:S(2)}) async-start(bf16[32,48,128]{2,1,0:T(8,128)(2,1)} %shard_map.76), calls=%async_computation.1 | async-start | bytes 786432 | tf_op jit(solution)/shard_map/all_to_all | solution.py:342
  45.1 2.4 %collective-permute-start.2 = (bf16[256,2176]{1,0:T(8,128)(2,1)S(1)}, bf16[256,2176]{1,0:T(8,128)(2,1)S(1)}, u32[]{:S(2)}, u32[]{:S(2)}) collective-permute-start(bf16[256,2176]{1,0:T(8,128)(2,1)S(1)} %bitcast.14), channel_id=1, source_target_pairs={{0,1},{1,0},{2,3},{3,2},{4,5},{5,4},{6,7},{7,6},{8,9},{9,8},{10,11... | collective-permute-start | bytes 3342344 | tf_op jit(solution)/shard_map/ppermute | solution.py:345
  47.5 0.0 copy-done.1
  47.5 0.0 copy-done.2
  47.6 0.8 shard_map.74
  48.3 11.5 %all-to-all-done.1.parts_ref = bf16[32,48,128]{2,1,0:T(8,128)(2,1)S(1)} async-done(((bf16[32,48,128]{2,1,0:T(8,128)(2,1)}), bf16[32,48,128]{2,1,0:T(8,128)(2,1)S(1)}, u32[]{:S(2)}, u32[]{:S(2)}) %all-to-all-start.1) | async-done | bytes 393248 | tf_op jit(solution)/shard_map/all_to_all | solution.py:342
  59.8 0.2 shard_map.77
  60.0 11.7 %all_to_all.20.pieces_ref = f32[8,32,128]{2,1,0:T(8,128)S(1)} all-to-all(f32[8,32,128]{2,1,0:T(8,128)S(1)} %shard_map.77), channel_id=1, replica_groups=mesh['zh'=4,'y'=8,'core'=2,'x'=4,'zl'=2] {'x','core'}, dimensions={0} | all-to-all | bytes 262144 | tf_op jit(solution)/shard_map/all_to_all | solution.py:347
  71.7 3.5 %shard_map.78 = bf16[32,2,8,128]{3,2,1,0:T(8,128)(2,1)S(1)} custom-call(bf16[1024,128]{1,0:T(8,128)(2,1)S(1)} %get-tuple-element.10.runs_ref, bf16[4,128,512]{2,1,0:T(8,128)(2,1)S(1)} %get-tuple-element.11.new_ref, f32[8,32,128]{2,1,0:T(8,128)S(1)} %all_to_all.20.pieces_ref, f32[8,128]{1,0:T(8,128)S(1)} %get-tuple-element.14.after_ref.aux_ref), custom_call_target="tpu_custom_call" | custom-call | flops 268435456 | bytes 1048576 | tf_op jit(solution)/shard_map/pallas_call | solution.py:260
  75.2 16.8 %all_to_all.21 = bf16[64,8,128]{2,1,0:T(8,128)(2,1)S(1)} all-to-all(bf16[64,8,128]{2,1,0:T(8,128)(2,1)S(1)} %bitcast.19), channel_id=1, replica_groups=mesh['zh'=4,'y'=8,'core'=2,'x'=4,'zl'=2] {'zh','y','zl'}, dimensions={0} | all-to-all | bytes 262144 | tf_op jit(solution)/shard_map/all_to_all | solution.py:349
  92.0 3.9 %all_gather.11 = bf16[128,8,128]{2,1,0:T(8,128)(2,1)S(1)} all-gather(bf16[64,8,128]{2,1,0:T(8,128)(2,1)S(1)} %all_to_all.21), channel_id=1, replica_groups=mesh['zh'=4,'y'=8,'core'=2,'x'=4,'zl'=2] {'core'}, dimensions={0}, use_global_device_ids=true | all-gather | bytes 393216 | tf_op jit(solution)/shard_map/all_gather | solution.py:350
  95.9 0.0 collective-permute-done.2.refs_3_
  95.9 2.1 %shard_map.79 = bf16[256,2048]{1,0:T(8,128)(2,1)} custom-call(s32[5]{0:T(128)S(1)} %stack.23.where_ref.refs_0_, bf16[64,2,8,128]{3,2,1,0:T(8,128)(2,1)S(1)} %bitcast.18, bf16[256,2176]{1,0:T(8,128)(2,1)S(1)} %bitcast.16, bf16[256,2176]{1,0:T(8,128)(2,1)S(1)} %collective-permute-done.2.refs_3_), custom_call_target="tpu_custom_call" | custom-call | flops 536870912 | bytes 3145728 | tf_op jit(solution)/shard_map/pallas_call | solution.py:308
  (1 shorter events, 0.0 us)
Async XLA Ops:
  2.1 5.0 %copy-start = (bf16[128,2048]{1,0:T(8,128)(2,1)S(1)}, bf16[128,2048]{1,0:T(8,128)(2,1)}, u32[]{:S(2)}) copy-start(bf16[128,2048]{1,0:T(8,128)(2,1)} %refs_1_.1) | copy-start | bytes 1572868
  2.1 9.0 %copy-start.3 = (f32[1024,16]{0,1:T(8,128)S(1)}, f32[1024,16]{0,1:T(8,128)}, u32[]{:S(2)}) copy-start(f32[1024,16]{0,1:T(8,128)} %param.9) | copy-start | bytes 196612
  2.1 16.9 %all-to-all-start = ((bf16[4,64,2176]{2,1,0:T(8,128)(2,1)}), bf16[4,64,2176]{2,1,0:T(8,128)(2,1)S(1)}, u32[]{:S(2)}, u32[]{:S(2)}) async-start(bf16[4,64,2176]{2,1,0:T(8,128)(2,1)} %shard_map.73), calls=%async_computation | async-start | bytes 2228224 | tf_op jit(solution)/shard_map/all_to_all | solution.py:331
  7.0 12.0 %collective-permute-start = (bf16[128,2048]{1,0:T(8,128)(2,1)S(1)}, bf16[128,2048]{1,0:T(8,128)(2,1)S(1)}, u32[]{:S(2)}, u32[]{:S(2)}) collective-permute-start(bf16[128,2048]{1,0:T(8,128)(2,1)S(1)} %copy-done), channel_id=1, source_target_pairs={{0,1},{1,0},{2,3},{3,2},{4,5},{5,4},{6,7},{7,6},{8,9},{9,8},{10,11... | collective-permute-start | bytes 1572872 | tf_op jit(solution)/shard_map/ppermute | solution.py:330
  11.1 16.4 %collective-permute-start.1 = (bf16[16,1024]{1,0:T(8,128)(2,1)S(1)}, bf16[16,1024]{1,0:T(8,128)(2,1)S(1)}, u32[]{:S(2)}, u32[]{:S(2)}) collective-permute-start(bf16[16,1024]{1,0:T(8,128)(2,1)S(1)} %convert_bitcast_fusion), channel_id=1, source_target_pairs={{0,0},{2,128},{4,256},{6,384},{128,2},{130,130},{132,258},{134,386... | collective-permute-start | bytes 98312 | tf_op jit(solution)/shard_map/ppermute | solution.py:334
  20.1 27.4 %copy-start.1 = (f32[8,2048]{1,0:T(8,128)S(1)}, f32[8,2048]{1,0:T(8,128)}, u32[]{:S(2)}) copy-start(f32[8,2048]{1,0:T(8,128)} %new_ref.1) | copy-start | bytes 196612
  20.1 27.4 %copy-start.2 = (f32[8,1024]{1,0:T(8,128)S(1)}, f32[8,1024]{1,0:T(8,128)}, u32[]{:S(2)}) copy-start(f32[8,1024]{1,0:T(8,128)} %design_ref.1) | copy-start | bytes 98308
  28.9 30.9 %all-to-all-start.1 = ((bf16[32,48,128]{2,1,0:T(8,128)(2,1)}), bf16[32,48,128]{2,1,0:T(8,128)(2,1)S(1)}, u32[]{:S(2)}, u32[]{:S(2)}) async-start(bf16[32,48,128]{2,1,0:T(8,128)(2,1)} %shard_map.76), calls=%async_computation.1 | async-start | bytes 786432 | tf_op jit(solution)/shard_map/all_to_all | solution.py:342
  45.1 50.8 %collective-permute-start.2 = (bf16[256,2176]{1,0:T(8,128)(2,1)S(1)}, bf16[256,2176]{1,0:T(8,128)(2,1)S(1)}, u32[]{:S(2)}, u32[]{:S(2)}) collective-permute-start(bf16[256,2176]{1,0:T(8,128)(2,1)S(1)} %bitcast.14), channel_id=1, source_target_pairs={{0,1},{1,0},{2,3},{3,2},{4,5},{5,4},{6,7},{7,6},{8,9},{9,8},{10,11... | collective-permute-start | bytes 3342344 | tf_op jit(solution)/shard_map/ppermute | solution.py:345

commit v7 on v6

--- a/solution.py
+++ b/solution.py
@@ -18,7 +18,7 @@
 SMEM = pl.BlockSpec(memory_space=pltpu.SMEM)
 CELLS = 2048
 WIDE = CELLS + 128
-BOUNDS = (0, 768, 1280, 1792, 2048)
+BOUNDS = (0, 512, 1024, 1536, 2048)
 
 
 def params(mib):
@@ -151,7 +151,7 @@
                 piece = full[4 * core + block : 4 * core + block + 1, 128 * tile : 128 * tile + 128]
                 for peer in range(4):
                     row = 8 * block + tile
-                    out_ref[2 * peer + core, row : row + 1, :] = piece
+                    out_ref[4 * core + peer, row : row + 1, :] = piece
 
 
 def weights(parts, after):
@@ -344,7 +344,7 @@
     runs_feat, new_feat, aux = prepare(where, basis, design, new_settings)
     basis_other = lax.ppermute(basis, "zl", swap)
 
-    pieces = lax.all_to_all(weights(parts, aux), ("x", "core"), 0, 0, tiled=True)
+    pieces = lax.all_to_all(weights(parts, aux), ("core", "x"), 0, 0, tiled=True)
     pred = predict(runs_feat, new_feat, pieces, aux)
     pred = lax.all_to_all(pred.reshape(64, 8, 128), ("zh", "y", "zl"), 0, 0, tiled=True)
     pred = lax.all_gather(pred, "core", axis=0, tiled=True)

time: 98.5 us -> 98.1 us (level)
  no operation moved by 1% of the time
where the time goes in v7:
time: 98.1 us; the launch traced here: 97.6 us
  blocking collectives  39.3 us (40%)
  starting transfers between devices  28.3 us (29%)
  waiting for transfers between devices  18.6 us (19%)
  Pallas kernels  11.1 us (11%)
    all_to_all x1, blocking collectives, on_device(): lax.all_to_all(pred.reshape(64, 8, 128), ('zh', 'y', 'zl'), 0, 0, tiled=T...  16.8 us
    all_to_all x1, starting transfers between devices, on_device(): lax.all_to_all(slots(where, mine, theirs, block), ('zh', 'y'), 0, 0, tile...  16.3 us
    all_to_all x1, blocking collectives, on_device(): lax.all_to_all(weights(parts, aux), ('core', 'x'), 0, 0, tiled=True)  11.6 us
    all_to_all x1, waiting for transfers between devices, on_device(): lax.all_to_all(slots(where, mine, theirs, block), ('zh', 'y'), 0, 0, tile...  11.5 us
    all_gather x1, blocking collectives, on_device(): theirs = lax.all_gather(theirs, 'core', axis=0)  7.36 us
    ppermute x1, waiting for transfers between devices, on_device(): fields_other = lax.ppermute(fields_runs, 'zl', swap)  7.18 us
    all_to_all x1, starting transfers between devices, on_device(): lax.all_to_all(pack(eof_basis.T, lscale, variance.reshape(1, 64)), 'x', 0...  4.97 us
    ppermute x1, starting transfers between devices, on_device(): fields_other = lax.ppermute(fields_runs, 'zl', swap)  3.99 us
  transfers between devices with their start and end apart: 5, of which 2 were waited for; matrix products, arithmetic and copies ran while one was open for 0% of the time, Pallas kernels for 6%

profile of v7, /device:TPU:1, one launch (start us, length us, event | category | flops | bytes accessed | tf_op | source)
XLA Modules:
  0.0 97.6 jit_solution(13388305405122223869)
XLA Ops:
  0.0 2.1 %shard_map.73 = bf16[4,64,2176]{2,1,0:T(8,128)(2,1)} custom-call(bf16[64,2048]{1,0:T(8,128)(2,1)} %bitcast.20, f32[8,64]{1,0:T(8,128)} %lscale_ref.1, f32[1,64]{1,0:T(1,128)} %bitcast.21), custom_call_target="tpu_custom_call" | custom-call | bytes 1310720 | tf_op jit(solution)/shard_map/pallas_call | solution.py:50
  2.1 0.0 copy-start
  2.1 0.0 copy-start.3
  2.1 5.0 %all-to-all-start = ((bf16[4,64,2176]{2,1,0:T(8,128)(2,1)}), bf16[4,64,2176]{2,1,0:T(8,128)(2,1)S(1)}, u32[]{:S(2)}, u32[]{:S(2)}) async-start(bf16[4,64,2176]{2,1,0:T(8,128)(2,1)} %shard_map.73), calls=%async_computation | async-start | bytes 2228224 | tf_op jit(solution)/shard_map/all_to_all | solution.py:331
  7.0 0.0 copy-done
  7.0 4.0 %collective-permute-start = (bf16[128,2048]{1,0:T(8,128)(2,1)S(1)}, bf16[128,2048]{1,0:T(8,128)(2,1)S(1)}, u32[]{:S(2)}, u32[]{:S(2)}) collective-permute-start(bf16[128,2048]{1,0:T(8,128)(2,1)S(1)} %copy-done), channel_id=1, source_target_pairs={{0,1},{1,0},{2,3},{3,2},{4,5},{5,4},{6,7},{7,6},{8,9},{9,8},{10,11... | collective-permute-start | bytes 1572872 | tf_op jit(solution)/shard_map/ppermute | solution.py:330
  11.0 0.0 copy-done.3
  11.1 0.7 collective-permute-start.1
  11.7 0.1 stack.23.where_ref.refs_0_
  11.8 7.2 %collective-permute-done.refs_2_ = bf16[128,2048]{1,0:T(8,128)(2,1)S(1)} collective-permute-done((bf16[128,2048]{1,0:T(8,128)(2,1)S(1)}, bf16[128,2048]{1,0:T(8,128)(2,1)S(1)}, u32[]{:S(2)}, u32[]{:S(2)}) %collective-permute-start) | collective-permute-done | bytes 524320 | tf_op jit(solution)/shard_map/ppermute | solution.py:330
  19.0 0.0 all-to-all-done
  19.0 1.1 %shard_map.75 = (f32[256,128]{1,0:T(8,128)S(1)}, f32[256,128]{1,0:T(8,128)S(1)}) custom-call(s32[5]{0:T(128)S(1)} %stack.23.where_ref.refs_0_, bf16[128,2048]{1,0:T(8,128)(2,1)S(1)} %copy-done, bf16[128,2048]{1,0:T(8,128)(2,1)S(1)} %collective-permute-done.refs_2_, bf16[256,2176]{1,0:T(8,128)(2,1)S(1)} %bitcast.13), custom_call_target="tpu_custom_call" | custom-call | flops 268435456 | bytes 2097152 | tf_op jit(solution)/shard_map/pallas_call | solution.py:83
  20.1 0.0 copy-start.1
  20.1 0.0 copy-start.2
  20.1 7.4 %all-gather = f32[512,128]{1,0:T(8,128)S(1)} all-gather(f32[256,128]{1,0:T(8,128)S(1)} %get-tuple-element.13), channel_id=2, replica_groups=mesh['zh'=4,'y'=8,'core'=2,'x'=4,'zl'=2] {'core'}, dimensions={0}, use_global_device_ids=true | all-gather | bytes 393216 | tf_op jit(solution)/shard_map/all_gather | solution.py:341
  27.5 0.0 collective-permute-done.1.block_ref
  27.5 1.4 %shard_map.76 = bf16[32,48,128]{2,1,0:T(8,128)(2,1)} custom-call(s32[5]{0:T(128)S(1)} %stack.23.where_ref.refs_0_, f32[256,128]{1,0:T(8,128)S(1)} %get-tuple-element.12.mine_ref, f32[2,256,128]{2,1,0:T(8,128)S(1)} %bitcast.17, bf16[16,1024]{1,0:T(8,128)(2,1)S(1)} %collective-permute-done.1.block_ref), custom_call_target="tpu_custom_call" | custom-call | flops 1048576 | bytes 1048576 | tf_op jit(solution)/shard_map/pallas_call | solution.py:119
  28.9 16.3 %all-to-all-start.1 = ((bf16[32,48,128]{2,1,0:T(8,128)(2,1)}), bf16[32,48,128]{2,1,0:T(8,128)(2,1)S(1)}, u32[]{:S(2)}, u32[]{:S(2)}) async-start(bf16[32,48,128]{2,1,0:T(8,128)(2,1)} %shard_map.76), calls=%async_computation.1 | async-start | bytes 786432 | tf_op jit(solution)/shard_map/all_to_all | solution.py:342
  45.1 2.4 %collective-permute-start.2 = (bf16[256,2176]{1,0:T(8,128)(2,1)S(1)}, bf16[256,2176]{1,0:T(8,128)(2,1)S(1)}, u32[]{:S(2)}, u32[]{:S(2)}) collective-permute-start(bf16[256,2176]{1,0:T(8,128)(2,1)S(1)} %bitcast.14), channel_id=1, source_target_pairs={{0,1},{1,0},{2,3},{3,2},{4,5},{5,4},{6,7},{7,6},{8,9},{9,8},{10,11... | collective-permute-start | bytes 3342344 | tf_op jit(solution)/shard_map/ppermute | solution.py:345
  47.5 0.0 copy-done.1
  47.5 0.0 copy-done.2
  47.6 0.8 shard_map.74
  48.3 11.5 %all-to-all-done.1.parts_ref = bf16[32,48,128]{2,1,0:T(8,128)(2,1)S(1)} async-done(((bf16[32,48,128]{2,1,0:T(8,128)(2,1)}), bf16[32,48,128]{2,1,0:T(8,128)(2,1)S(1)}, u32[]{:S(2)}, u32[]{:S(2)}) %all-to-all-start.1) | async-done | bytes 393248 | tf_op jit(solution)/shard_map/all_to_all | solution.py:342
  59.8 0.2 shard_map.77
  60.0 11.6 %all_to_all.20.pieces_ref = f32[8,32,128]{2,1,0:T(8,128)S(1)} all-to-all(f32[8,32,128]{2,1,0:T(8,128)S(1)} %shard_map.77), channel_id=1, replica_groups=mesh['zh'=4,'y'=8,'core'=2,'x'=4,'zl'=2] {'core','x'}, dimensions={0} | all-to-all | bytes 262144 | tf_op jit(solution)/shard_map/all_to_all | solution.py:347
  71.6 3.5 %shard_map.78 = bf16[32,2,8,128]{3,2,1,0:T(8,128)(2,1)S(1)} custom-call(bf16[1024,128]{1,0:T(8,128)(2,1)S(1)} %get-tuple-element.10.runs_ref, bf16[4,128,512]{2,1,0:T(8,128)(2,1)S(1)} %get-tuple-element.11.new_ref, f32[8,32,128]{2,1,0:T(8,128)S(1)} %all_to_all.20.pieces_ref, f32[8,128]{1,0:T(8,128)S(1)} %get-tuple-element.14.after_ref.aux_ref), custom_call_target="tpu_custom_call" | custom-call | flops 268435456 | bytes 1048576 | tf_op jit(solution)/shard_map/pallas_call | solution.py:260
  75.1 16.8 %all_to_all.21 = bf16[64,8,128]{2,1,0:T(8,128)(2,1)S(1)} all-to-all(bf16[64,8,128]{2,1,0:T(8,128)(2,1)S(1)} %bitcast.19), channel_id=1, replica_groups=mesh['zh'=4,'y'=8,'core'=2,'x'=4,'zl'=2] {'zh','y','zl'}, dimensions={0} | all-to-all | bytes 262144 | tf_op jit(solution)/shard_map/all_to_all | solution.py:349
  91.9 3.5 %all_gather.11 = bf16[128,8,128]{2,1,0:T(8,128)(2,1)S(1)} all-gather(bf16[64,8,128]{2,1,0:T(8,128)(2,1)S(1)} %all_to_all.21), channel_id=1, replica_groups=mesh['zh'=4,'y'=8,'core'=2,'x'=4,'zl'=2] {'core'}, dimensions={0}, use_global_device_ids=true | all-gather | bytes 393216 | tf_op jit(solution)/shard_map/all_gather | solution.py:350
  95.5 0.0 collective-permute-done.2.refs_3_
  95.5 2.1 %shard_map.79 = bf16[256,2048]{1,0:T(8,128)(2,1)} custom-call(s32[5]{0:T(128)S(1)} %stack.23.where_ref.refs_0_, bf16[64,2,8,128]{3,2,1,0:T(8,128)(2,1)S(1)} %bitcast.18, bf16[256,2176]{1,0:T(8,128)(2,1)S(1)} %bitcast.16, bf16[256,2176]{1,0:T(8,128)(2,1)S(1)} %collective-permute-done.2.refs_3_), custom_call_target="tpu_custom_call" | custom-call | flops 536870912 | bytes 3145728 | tf_op jit(solution)/shard_map/pallas_call | solution.py:308
  (1 shorter events, 0.0 us)
Async XLA Ops:
  2.1 5.0 %copy-start = (bf16[128,2048]{1,0:T(8,128)(2,1)S(1)}, bf16[128,2048]{1,0:T(8,128)(2,1)}, u32[]{:S(2)}) copy-start(bf16[128,2048]{1,0:T(8,128)(2,1)} %refs_1_.1) | copy-start | bytes 1572868
  2.1 9.0 %copy-start.3 = (f32[1024,16]{0,1:T(8,128)S(1)}, f32[1024,16]{0,1:T(8,128)}, u32[]{:S(2)}) copy-start(f32[1024,16]{0,1:T(8,128)} %param.9) | copy-start | bytes 196612
  2.1 16.9 %all-to-all-start = ((bf16[4,64,2176]{2,1,0:T(8,128)(2,1)}), bf16[4,64,2176]{2,1,0:T(8,128)(2,1)S(1)}, u32[]{:S(2)}, u32[]{:S(2)}) async-start(bf16[4,64,2176]{2,1,0:T(8,128)(2,1)} %shard_map.73), calls=%async_computation | async-start | bytes 2228224 | tf_op jit(solution)/shard_map/all_to_all | solution.py:331
  7.0 12.0 %collective-permute-start = (bf16[128,2048]{1,0:T(8,128)(2,1)S(1)}, bf16[128,2048]{1,0:T(8,128)(2,1)S(1)}, u32[]{:S(2)}, u32[]{:S(2)}) collective-permute-start(bf16[128,2048]{1,0:T(8,128)(2,1)S(1)} %copy-done), channel_id=1, source_target_pairs={{0,1},{1,0},{2,3},{3,2},{4,5},{5,4},{6,7},{7,6},{8,9},{9,8},{10,11... | collective-permute-start | bytes 1572872 | tf_op jit(solution)/shard_map/ppermute | solution.py:330
  11.1 16.4 %collective-permute-start.1 = (bf16[16,1024]{1,0:T(8,128)(2,1)S(1)}, bf16[16,1024]{1,0:T(8,128)(2,1)S(1)}, u32[]{:S(2)}, u32[]{:S(2)}) collective-permute-start(bf16[16,1024]{1,0:T(8,128)(2,1)S(1)} %convert_bitcast_fusion), channel_id=1, source_target_pairs={{0,0},{2,128},{4,256},{6,384},{128,2},{130,130},{132,258},{134,386... | collective-permute-start | bytes 98312 | tf_op jit(solution)/shard_map/ppermute | solution.py:334
  20.1 27.4 %copy-start.1 = (f32[8,2048]{1,0:T(8,128)S(1)}, f32[8,2048]{1,0:T(8,128)}, u32[]{:S(2)}) copy-start(f32[8,2048]{1,0:T(8,128)} %new_ref.1) | copy-start | bytes 196612
  20.1 27.4 %copy-start.2 = (f32[8,1024]{1,0:T(8,128)S(1)}, f32[8,1024]{1,0:T(8,128)}, u32[]{:S(2)}) copy-start(f32[8,1024]{1,0:T(8,128)} %design_ref.1) | copy-start | bytes 98308
  28.9 30.9 %all-to-all-start.1 = ((bf16[32,48,128]{2,1,0:T(8,128)(2,1)}), bf16[32,48,128]{2,1,0:T(8,128)(2,1)S(1)}, u32[]{:S(2)}, u32[]{:S(2)}) async-start(bf16[32,48,128]{2,1,0:T(8,128)(2,1)} %shard_map.76), calls=%async_computation.1 | async-start | bytes 786432 | tf_op jit(solution)/shard_map/all_to_all | solution.py:342
  45.1 50.4 %collective-permute-start.2 = (bf16[256,2176]{1,0:T(8,128)(2,1)S(1)}, bf16[256,2176]{1,0:T(8,128)(2,1)S(1)}, u32[]{:S(2)}, u32[]{:S(2)}) collective-permute-start(bf16[256,2176]{1,0:T(8,128)(2,1)S(1)} %bitcast.14), channel_id=1, source_target_pairs={{0,1},{1,0},{2,3},{3,2},{4,5},{5,4},{6,7},{7,6},{8,9},{9,8},{10,11... | collective-permute-start | bytes 3342344 | tf_op jit(solution)/shard_map/ppermute | solution.py:345
